TPU v7x, 32 devices: a whole 2x2x4 slice. The times are simulated.
32 devices in a mesh: dp: 2 (over x), seq: 4 (over y, core), expert: 4 (over z).
Axes of the slice: x: 2, y: 2, z: 4, core: 2. Of those that a mesh axis runs over, the one named last changes fastest.
Arguments:
- tokens: bfloat16 [8, 1024, 768], P(('dp', 'expert'), 'seq'), may hold values from -6 to 6
- qkv_weight: bfloat16 [768, 2304], P(('dp', 'seq', 'expert')), may hold values from -0.21875 to 0.21875
- out_weight: bfloat16 [768, 768], P(('dp', 'seq', 'expert')), may hold values from -1.75 to 1.75
- router_weight: bfloat16 [768, 4], P(('dp', 'seq', 'expert')), may hold values from -0.15625 to 0.15625
- w_in: bfloat16 [4, 768, 3072], P('expert', ('dp', 'seq')), may hold values from -0.21875 to 0.21875
- w_out: bfloat16 [4, 3072, 768], P('expert', None, ('dp', 'seq')), may hold values from -0.109375 to 0.109375
- norm_gains: float32 [2, 768], replicated, may hold values from 0.5 to 1.5
- bias_table: float32 [32, 12], replicated, may hold values from -4 to 4
- expert_ids: int32 [8, 1024, 2], P(('dp', 'expert'), 'seq'), may hold values from 0 to 3, all different within a row; in each aligned block of 256 rows (0 to 255, 256 to 511, ..., all dimensions but the last counted through in order) at most 192 rows name the same one
- cotangent: bfloat16 [8, 1024, 768], P(('dp', 'expert'), 'seq'), may hold values from -6 to 6
Outputs:
- layer_out: bfloat16 [8, 1024, 768], P(('dp', 'expert'), 'seq')
- input_grad: bfloat16 [8, 1024, 768], P(('dp', 'expert'), 'seq')
- qkv_grad: float32 [768, 2304], P(('dp', 'seq', 'expert'))
- out_grad: float32 [768, 768], P(('dp', 'seq', 'expert'))
- router_grad: float32 [768, 4], P(('dp', 'seq', 'expert'))
- w_in_grad: float32 [4, 768, 3072], P('expert', ('dp', 'seq'))
- w_out_grad: float32 [4, 3072, 768], P('expert', None, ('dp', 'seq'))
- gains_grad: float32 [2, 768], replicated
- table_grad: float32 [32, 12], replicated
Inputs may be any that keep to these rules, and one draw needn't show every extreme that they name: `expert_ids`: the two experts of a token differ. Within the 256 rows of one device (aligned blocks of 256 positions of a sequence) no expert is named more than 192 times, a bound that some block reaches.
All inputs are finite; a program needn't handle non-finite values.
Results may differ from a plain program's by a relative error of at most 0.015.
Values may be sent and summed in bfloat16 or wider, within the bound.
A program may use at most 128 MiB of HBM per device.

v0:
```python
import math

import jax
import jax.numpy as jnp
from jax import lax
from jax.sharding import PartitionSpec as P

D = 768
HEADS = 12
HEAD_DIM = 64
FF = 3072
BUCKETS = 32
LEN_DEV = 256


EPS = 1e-06
HIGH_PRECISION = lax.Precision.HIGHEST
CONTRACT_ROWS = (((0,), (0,)), ((), ()))


def bucket_edges(bucket_count):
    exact_count = bucket_count // 2
    boundaries = list(range(1, exact_count + 1))
    for bucket_index in range(exact_count + 1, bucket_count):
        power = (bucket_index - exact_count) / (bucket_count - exact_count)
        boundaries.append(math.ceil(exact_count * (128.0 / exact_count) ** power))
    return boundaries


def bucket_ids(distance, bucket_count):
    distance = jnp.maximum(distance, 0)
    bucket_sum = jnp.zeros(distance.shape, jnp.int32)
    for boundary in bucket_edges(bucket_count):
        bucket_sum = bucket_sum + (distance >= boundary).astype(jnp.int32)
    return bucket_sum


def norm_forward(values, scale_gain):
    inverse = lax.rsqrt(jnp.mean(values * values, axis=-1, keepdims=True) + EPS)
    normal_rows = values * inverse
    return (normal_rows * scale_gain, normal_rows, inverse)


def norm_backward(grad_out, normal_rows, inverse, scale_gain):
    gain_part = jnp.sum(grad_out * normal_rows, axis=0)
    scaled = grad_out * scale_gain
    value_grad = inverse * (
        scaled - normal_rows * jnp.mean(scaled * normal_rows, axis=-1, keepdims=True)
    )
    return (value_grad, gain_part)


def split_heads(matrix):
    return matrix.reshape(matrix.shape[0], HEADS, HEAD_DIM).transpose(1, 0, 2)


def join_heads(stacked):
    return stacked.transpose(1, 0, 2).reshape(stacked.shape[1], HEADS * HEAD_DIM)


def to_slots(slot_table, rows):
    return jnp.dot(slot_table, rows, preferred_element_type=jnp.float32).astype(jnp.bfloat16)


def from_slots(slot_table, rows):
    return lax.dot_general(slot_table, rows, CONTRACT_ROWS, preferred_element_type=jnp.float32)


def local(
    tokens,
    qkv_weight,
    out_weight,
    router_weight,
    w_in,
    w_out,
    norm_gains,
    bias_table,
    expert_ids,
    cotangent,
):
    inputs = tokens[0].astype(jnp.float32)
    full_length = LEN_DEV * lax.axis_size("seq")
    experts_total = lax.axis_size("expert")
    capacity = 3 * LEN_DEV // experts_total
    score_scale = HEAD_DIM ** (-0.5)
    qkv_full, out_full, router_full = (
        lax.all_gather(qkv_weight, ("dp", "seq", "expert"), axis=0, tiled=True),
        lax.all_gather(out_weight, ("dp", "seq", "expert"), axis=0, tiled=True),
        lax.all_gather(router_weight, ("dp", "seq", "expert"), axis=0, tiled=True),
    )
    normalized_rows, normal_one, inverse_one = norm_forward(inputs, norm_gains[0])
    normed_low = normalized_rows.astype(jnp.bfloat16)
    projected_rows = jnp.dot(normed_low, qkv_full, preferred_element_type=jnp.float32).astype(
        jnp.bfloat16
    )
    key_values = lax.all_gather(projected_rows[:, D:], "seq", axis=0, tiled=True)
    query_pos = lax.axis_index("seq") * LEN_DEV + jnp.arange(LEN_DEV, dtype=jnp.int32)
    key_pos = jnp.arange(full_length, dtype=jnp.int32)
    distance = query_pos[:, None] - key_pos[None, :]
    causal = distance >= 0
    buckets = bucket_ids(distance, BUCKETS)
    bucket_onehot = (buckets[..., None] == jnp.arange(BUCKETS, dtype=jnp.int32)).astype(
        jnp.bfloat16
    )
    queries = split_heads(projected_rows[:, :D])
    key_heads = split_heads(key_values[:, :D])
    value_heads = split_heads(key_values[:, D:])
    columns = bias_table.T

    def head_scores(queries_one, keys_one, column):
        raw_scores = jnp.einsum(
            "qd,kd->qk", queries_one, keys_one, preferred_element_type=jnp.float32
        )
        raw_scores = raw_scores * score_scale + jnp.take(column, buckets)
        return jnp.where(causal, raw_scores, -1e30)

    def head_forward(operands):
        queries_one, keys_one, values_one, column = operands
        scores = head_scores(queries_one, keys_one, column)
        row_peak = jnp.max(scores, axis=-1, keepdims=True)
        weights_exp = jnp.exp(scores - row_peak)
        total_weight = jnp.sum(weights_exp, axis=-1, keepdims=True)
        prob_low = (weights_exp / total_weight).astype(jnp.bfloat16)
        result = jnp.dot(prob_low, values_one, preferred_element_type=jnp.float32)
        return (result, (row_peak + jnp.log(total_weight))[:, 0])

    attention_result, log_totals = lax.map(head_forward, (queries, key_heads, value_heads, columns))
    attended_low = join_heads(attention_result).astype(jnp.bfloat16)
    middle = inputs + jnp.dot(attended_low, out_full, preferred_element_type=jnp.float32)
    mixed, normal_two, inverse_two = norm_forward(middle, norm_gains[1])
    mixed_low = mixed.astype(jnp.bfloat16)
    router_logits = jnp.dot(mixed_low, router_full, preferred_element_type=jnp.float32)
    route_ids = expert_ids[0]
    choose = (route_ids[..., None] == jnp.arange(experts_total, dtype=jnp.int32)).astype(
        jnp.float32
    )
    chosen = jnp.sum(choose * router_logits[:, None, :], axis=-1)
    gate_weights = jax.nn.softmax(chosen, axis=-1)
    flat_ids = route_ids.reshape(-1)
    expert_hits = (flat_ids[:, None] == jnp.arange(experts_total, dtype=jnp.int32)).astype(
        jnp.int32
    )
    slot_rank = jnp.sum((jnp.cumsum(expert_hits, axis=0) - 1) * expert_hits, axis=-1)
    places = flat_ids * capacity + slot_rank
    slot_index = jnp.arange(experts_total * capacity, dtype=jnp.int32)
    slot_table = (slot_index[:, None] == places[None, :]).astype(jnp.bfloat16)
    copies = jnp.broadcast_to(mixed_low[:, None, :], (LEN_DEV, 2, D)).reshape(LEN_DEV * 2, D)
    outgoing = to_slots(slot_table, copies)
    arrived = lax.all_to_all(
        outgoing.reshape(experts_total, capacity, D),
        "expert",
        split_axis=0,
        concat_axis=0,
        tiled=True,
    )
    expert_rows = arrived.reshape(experts_total * capacity, D)
    w_in_full, w_out_full = (
        lax.all_gather(w_in, ("dp", "seq"), axis=1, tiled=True),
        lax.all_gather(w_out, ("dp", "seq"), axis=2, tiled=True),
    )
    pre_act = jnp.dot(expert_rows, w_in_full[0], preferred_element_type=jnp.float32)
    hidden_low = jax.nn.gelu(pre_act).astype(jnp.bfloat16)
    expert_out = jnp.dot(hidden_low, w_out_full[0], preferred_element_type=jnp.float32).astype(
        jnp.bfloat16
    )
    returned = lax.all_to_all(
        expert_out.reshape(experts_total, capacity, D),
        "expert",
        split_axis=0,
        concat_axis=0,
        tiled=True,
    )
    gathered_rows = from_slots(slot_table, returned.reshape(experts_total * capacity, D)).reshape(
        LEN_DEV, 2, D
    )
    block_out = middle + jnp.sum(gate_weights[..., None] * gathered_rows, axis=1)
    layer_out = block_out.astype(jnp.bfloat16)[None]
    upstream = cotangent[0].astype(jnp.float32)
    gate_grad = jnp.sum(upstream[:, None, :] * gathered_rows, axis=-1)
    copy_grad = (
        (gate_weights[..., None] * upstream[:, None, :])
        .astype(jnp.bfloat16)
        .reshape(LEN_DEV * 2, D)
    )
    outgoing_grad = to_slots(slot_table, copy_grad)
    arrived_grad = lax.all_to_all(
        outgoing_grad.reshape(experts_total, capacity, D),
        "expert",
        split_axis=0,
        concat_axis=0,
        tiled=True,
    )
    arrived_grad = arrived_grad.reshape(experts_total * capacity, D)
    w_in_back, w_out_back = (
        lax.all_gather(w_in, ("dp", "seq"), axis=1, tiled=True),
        lax.all_gather(w_out, ("dp", "seq"), axis=2, tiled=True),
    )
    hidden_grad = jnp.einsum(
        "rd,fd->rf", arrived_grad, w_out_back[0], preferred_element_type=jnp.float32
    )
    gelu_value, gelu_pull = jax.vjp(jax.nn.gelu, pre_act)
    pre_grad = gelu_pull(hidden_grad)[0].astype(jnp.bfloat16)
    row_grad = jnp.einsum(
        "rf,df->rd", pre_grad, w_in_back[0], preferred_element_type=jnp.float32
    ).astype(jnp.bfloat16)
    returned_grad = lax.all_to_all(
        row_grad.reshape(experts_total, capacity, D),
        "expert",
        split_axis=0,
        concat_axis=0,
        tiled=True,
    )
    copy_back = from_slots(slot_table, returned_grad.reshape(experts_total * capacity, D))
    copy_back = jnp.sum(copy_back.reshape(LEN_DEV, 2, D), axis=1)
    first_term = lax.dot_general(
        expert_rows, pre_grad, CONTRACT_ROWS, preferred_element_type=jnp.float32
    )
    second_term = lax.dot_general(
        arrived_grad, hidden_low, CONTRACT_ROWS, preferred_element_type=jnp.float32
    )
    expert_grad = lax.psum_scatter(
        jnp.concatenate([first_term, second_term], axis=1).astype(jnp.bfloat16),
        ("dp", "seq"),
        scatter_dimension=0,
        tiled=True,
    ).astype(jnp.float32)
    w_in_grad = expert_grad[:, :FF][None]
    w_out_grad = expert_grad[:, FF:].T[None]
    qkv_back, out_back, router_back = (
        lax.all_gather(qkv_weight, ("dp", "seq", "expert"), axis=0, tiled=True),
        lax.all_gather(out_weight, ("dp", "seq", "expert"), axis=0, tiled=True),
        lax.all_gather(router_weight, ("dp", "seq", "expert"), axis=0, tiled=True),
    )
    gate_mean = jnp.sum(gate_weights * gate_grad, axis=-1, keepdims=True)
    chosen_grad = gate_weights * (gate_grad - gate_mean)
    logit_grad = jnp.sum(choose * chosen_grad[..., None], axis=1)
    router_part = lax.dot_general(
        mixed_low.astype(jnp.float32), logit_grad, CONTRACT_ROWS, precision=HIGH_PRECISION
    )
    mixed_grad = copy_back + jnp.dot(
        logit_grad, router_back.astype(jnp.float32).T, precision=HIGH_PRECISION
    )
    middle_norm_grad, gain_two = norm_backward(mixed_grad, normal_two, inverse_two, norm_gains[1])
    middle_grad = upstream + middle_norm_grad
    branch_low = middle_grad.astype(jnp.bfloat16)
    out_part = lax.dot_general(
        attended_low, branch_low, CONTRACT_ROWS, preferred_element_type=jnp.float32
    )
    attended_grad = jnp.einsum(
        "qe,de->qd", branch_low, out_back, preferred_element_type=jnp.float32
    ).astype(jnp.bfloat16)
    grad_heads = split_heads(attended_grad)

    def head_backward(operands):
        queries_one, keys_one, values_one, column, log_total, grad_one = operands
        scores = head_scores(queries_one, keys_one, column)
        probabilities = jnp.exp(scores - log_total[:, None])
        prob_low = probabilities.astype(jnp.bfloat16)
        prob_grad = jnp.einsum(
            "qd,kd->qk", grad_one, values_one, preferred_element_type=jnp.float32
        )
        row_dot = jnp.sum(probabilities * prob_grad, axis=-1, keepdims=True)
        score_grad = (probabilities * (prob_grad - row_dot)).astype(jnp.bfloat16)
        query_grad = jnp.dot(score_grad, keys_one, preferred_element_type=jnp.float32) * score_scale
        key_grad = (
            lax.dot_general(
                score_grad, queries_one, CONTRACT_ROWS, preferred_element_type=jnp.float32
            )
            * score_scale
        )
        value_grad = lax.dot_general(
            prob_low, grad_one, CONTRACT_ROWS, preferred_element_type=jnp.float32
        )
        column_grad = jnp.einsum(
            "qk,qkb->b", score_grad, bucket_onehot, preferred_element_type=jnp.float32
        )
        return (query_grad, key_grad, value_grad, column_grad)

    query_grads, key_grads, value_grads, column_grads = lax.map(
        head_backward, (queries, key_heads, value_heads, columns, log_totals, grad_heads)
    )
    kv_part = jnp.concatenate([join_heads(key_grads), join_heads(value_grads)], axis=1)
    kv_grad = lax.psum_scatter(
        kv_part.astype(jnp.bfloat16), "seq", scatter_dimension=0, tiled=True
    ).astype(jnp.float32)
    projected_grad = jnp.concatenate([join_heads(query_grads), kv_grad], axis=1).astype(
        jnp.bfloat16
    )
    qkv_part = lax.dot_general(
        normed_low, projected_grad, CONTRACT_ROWS, preferred_element_type=jnp.float32
    )
    normed_grad = jnp.einsum(
        "qe,de->qd", projected_grad, qkv_back, preferred_element_type=jnp.float32
    )
    input_norm_grad, gain_one = norm_backward(normed_grad, normal_one, inverse_one, norm_gains[0])
    input_grad = (middle_grad + input_norm_grad).astype(jnp.bfloat16)[None]
    qkv_grad, out_grad, router_grad = (
        lax.psum_scatter(qkv_part, ("dp", "seq", "expert"), scatter_dimension=0, tiled=True),
        lax.psum_scatter(out_part, ("dp", "seq", "expert"), scatter_dimension=0, tiled=True),
        lax.psum_scatter(router_part, ("dp", "seq", "expert"), scatter_dimension=0, tiled=True),
    )
    gains_grad, table_grad = lax.psum(
        (jnp.stack([gain_one, gain_two]), column_grads.T), ("dp", "seq", "expert")
    )
    return (
        layer_out,
        input_grad,
        qkv_grad,
        out_grad,
        router_grad,
        w_in_grad,
        w_out_grad,
        gains_grad,
        table_grad,
    )


def solution(mesh):
    return jax.shard_map(
        local,
        mesh=mesh,
        in_specs=(
            P(("dp", "expert"), "seq", None),
            P(("dp", "seq", "expert"), None),
            P(("dp", "seq", "expert"), None),
            P(("dp", "seq", "expert"), None),
            P("expert", ("dp", "seq"), None),
            P("expert", None, ("dp", "seq")),
            P(),
            P(),
            P(("dp", "expert"), "seq", None),
            P(("dp", "expert"), "seq", None),
        ),
        out_specs=(
            P(("dp", "expert"), "seq", None),
            P(("dp", "expert"), "seq", None),
            P(("dp", "seq", "expert"), None),
            P(("dp", "seq", "expert"), None),
            P(("dp", "seq", "expert"), None),
            P("expert", ("dp", "seq"), None),
            P("expert", None, ("dp", "seq")),
            P(),
            P(),
        ),
        check_vma=False,
    )
```

profile of v0, /device:TPU:0, one launch (start us, length us, event | category | flops | bytes accessed | tf_op | source)
XLA Modules:
  0.0 1537.6 jit_solution(1096647247927112004)
XLA Ops:
  9.9 63.9 %all-gather.7.cloned.1.call-done = bf16[768,2304]{1,0:T(8,128)(2,1)} async-done(((bf16[24,2304]{1,0:T(8,128)(2,1)}), bf16[768,2304]{1,0:T(8,128)(2,1)}) %all-gather.7.cloned.1.call-update) | async-done | bytes 3538960 | tf_op jit(solution)/shard_map/all_gather | solution.py:87
  121.1 356.5 %while.31 = (s32[]{:T(128)}, bf16[12,256,64]{1,2,0:T(8,128)(2,1)}, f32[12,256]{1,0:T(8,128)}, bf16[12,256,64]{2,1,0:T(8,128)(2,1)}, bf16[12,1024,64]{2,1,0:T(8,1...) while((s32[]{:T(128)}, bf16[12,256,64]{1,2,0:T(8,128)(2,1)}, ...), condition=%wide.region_4.6_spmd.clone, body=%wide.region_1.5_spmd.clone.sunk | while | flops 88080128 | bytes 4879997 | solution.py:127
  123.3 24.0 %fusion.212 = (f32[256]{0:T(256)S(1)}, f32[256,1024]{1,0:T(8,128)S(1)}) fusion(f32[]{:T(128)} %bitcast.342, f32[]{:T(128)} %bitcast.343, f32[]{:T(128)} %bitcast.344, f32[]{:T(128)} %bitcast.345, f32[]{:T(128)} %bitcast.346, f32[]{:T(128)} %bitcast.347, f32[]{:T(128)} %bitcast.348, f32[]{:T(128)} %bitcast.349, f32[]{:T(128)} %bitcast.350, ...), kind=kOutput, calls=%fused_computation.211.clone.1 | convolution fusion | flops 53214976 | bytes 2444288 | tf_op jit(solution)/shard_map/while/body/eval_jaxpr/qd,kd->qk/dot_general | solution.py:111
  153.0 24.0 %fusion.212 = (f32[256]{0:T(256)S(1)}, f32[256,1024]{1,0:T(8,128)S(1)}) fusion(f32[]{:T(128)} %bitcast.342, f32[]{:T(128)} %bitcast.343, f32[]{:T(128)} %bitcast.344, f32[]{:T(128)} %bitcast.345, f32[]{:T(128)} %bitcast.346, f32[]{:T(128)} %bitcast.347, f32[]{:T(128)} %bitcast.348, f32[]{:T(128)} %bitcast.349, f32[]{:T(128)} %bitcast.350, ...), kind=kOutput, calls=%fused_computation.211.clone.1 | convolution fusion | flops 53214976 | bytes 2444288 | tf_op jit(solution)/shard_map/while/body/eval_jaxpr/qd,kd->qk/dot_general | solution.py:111
  182.7 24.0 %fusion.212 = (f32[256]{0:T(256)S(1)}, f32[256,1024]{1,0:T(8,128)S(1)}) fusion(f32[]{:T(128)} %bitcast.342, f32[]{:T(128)} %bitcast.343, f32[]{:T(128)} %bitcast.344, f32[]{:T(128)} %bitcast.345, f32[]{:T(128)} %bitcast.346, f32[]{:T(128)} %bitcast.347, f32[]{:T(128)} %bitcast.348, f32[]{:T(128)} %bitcast.349, f32[]{:T(128)} %bitcast.350, ...), kind=kOutput, calls=%fused_computation.211.clone.1 | convolution fusion | flops 53214976 | bytes 2444288 | tf_op jit(solution)/shard_map/while/body/eval_jaxpr/qd,kd->qk/dot_general | solution.py:111
  212.4 24.0 %fusion.212 = (f32[256]{0:T(256)S(1)}, f32[256,1024]{1,0:T(8,128)S(1)}) fusion(f32[]{:T(128)} %bitcast.342, f32[]{:T(128)} %bitcast.343, f32[]{:T(128)} %bitcast.344, f32[]{:T(128)} %bitcast.345, f32[]{:T(128)} %bitcast.346, f32[]{:T(128)} %bitcast.347, f32[]{:T(128)} %bitcast.348, f32[]{:T(128)} %bitcast.349, f32[]{:T(128)} %bitcast.350, ...), kind=kOutput, calls=%fused_computation.211.clone.1 | convolution fusion | flops 53214976 | bytes 2444288 | tf_op jit(solution)/shard_map/while/body/eval_jaxpr/qd,kd->qk/dot_general | solution.py:111
  242.2 24.0 %fusion.212 = (f32[256]{0:T(256)S(1)}, f32[256,1024]{1,0:T(8,128)S(1)}) fusion(f32[]{:T(128)} %bitcast.342, f32[]{:T(128)} %bitcast.343, f32[]{:T(128)} %bitcast.344, f32[]{:T(128)} %bitcast.345, f32[]{:T(128)} %bitcast.346, f32[]{:T(128)} %bitcast.347, f32[]{:T(128)} %bitcast.348, f32[]{:T(128)} %bitcast.349, f32[]{:T(128)} %bitcast.350, ...), kind=kOutput, calls=%fused_computation.211.clone.1 | convolution fusion | flops 53214976 | bytes 2444288 | tf_op jit(solution)/shard_map/while/body/eval_jaxpr/qd,kd->qk/dot_general | solution.py:111
  271.9 24.0 %fusion.212 = (f32[256]{0:T(256)S(1)}, f32[256,1024]{1,0:T(8,128)S(1)}) fusion(f32[]{:T(128)} %bitcast.342, f32[]{:T(128)} %bitcast.343, f32[]{:T(128)} %bitcast.344, f32[]{:T(128)} %bitcast.345, f32[]{:T(128)} %bitcast.346, f32[]{:T(128)} %bitcast.347, f32[]{:T(128)} %bitcast.348, f32[]{:T(128)} %bitcast.349, f32[]{:T(128)} %bitcast.350, ...), kind=kOutput, calls=%fused_computation.211.clone.1 | convolution fusion | flops 53214976 | bytes 2444288 | tf_op jit(solution)/shard_map/while/body/eval_jaxpr/qd,kd->qk/dot_general | solution.py:111
  301.6 24.0 %fusion.212 = (f32[256]{0:T(256)S(1)}, f32[256,1024]{1,0:T(8,128)S(1)}) fusion(f32[]{:T(128)} %bitcast.342, f32[]{:T(128)} %bitcast.343, f32[]{:T(128)} %bitcast.344, f32[]{:T(128)} %bitcast.345, f32[]{:T(128)} %bitcast.346, f32[]{:T(128)} %bitcast.347, f32[]{:T(128)} %bitcast.348, f32[]{:T(128)} %bitcast.349, f32[]{:T(128)} %bitcast.350, ...), kind=kOutput, calls=%fused_computation.211.clone.1 | convolution fusion | flops 53214976 | bytes 2444288 | tf_op jit(solution)/shard_map/while/body/eval_jaxpr/qd,kd->qk/dot_general | solution.py:111
  331.3 24.0 %fusion.212 = (f32[256]{0:T(256)S(1)}, f32[256,1024]{1,0:T(8,128)S(1)}) fusion(f32[]{:T(128)} %bitcast.342, f32[]{:T(128)} %bitcast.343, f32[]{:T(128)} %bitcast.344, f32[]{:T(128)} %bitcast.345, f32[]{:T(128)} %bitcast.346, f32[]{:T(128)} %bitcast.347, f32[]{:T(128)} %bitcast.348, f32[]{:T(128)} %bitcast.349, f32[]{:T(128)} %bitcast.350, ...), kind=kOutput, calls=%fused_computation.211.clone.1 | convolution fusion | flops 53214976 | bytes 2444288 | tf_op jit(solution)/shard_map/while/body/eval_jaxpr/qd,kd->qk/dot_general | solution.py:111
  361.0 24.0 %fusion.212 = (f32[256]{0:T(256)S(1)}, f32[256,1024]{1,0:T(8,128)S(1)}) fusion(f32[]{:T(128)} %bitcast.342, f32[]{:T(128)} %bitcast.343, f32[]{:T(128)} %bitcast.344, f32[]{:T(128)} %bitcast.345, f32[]{:T(128)} %bitcast.346, f32[]{:T(128)} %bitcast.347, f32[]{:T(128)} %bitcast.348, f32[]{:T(128)} %bitcast.349, f32[]{:T(128)} %bitcast.350, ...), kind=kOutput, calls=%fused_computation.211.clone.1 | convolution fusion | flops 53214976 | bytes 2444288 | tf_op jit(solution)/shard_map/while/body/eval_jaxpr/qd,kd->qk/dot_general | solution.py:111
  390.7 24.0 %fusion.212 = (f32[256]{0:T(256)S(1)}, f32[256,1024]{1,0:T(8,128)S(1)}) fusion(f32[]{:T(128)} %bitcast.342, f32[]{:T(128)} %bitcast.343, f32[]{:T(128)} %bitcast.344, f32[]{:T(128)} %bitcast.345, f32[]{:T(128)} %bitcast.346, f32[]{:T(128)} %bitcast.347, f32[]{:T(128)} %bitcast.348, f32[]{:T(128)} %bitcast.349, f32[]{:T(128)} %bitcast.350, ...), kind=kOutput, calls=%fused_computation.211.clone.1 | convolution fusion | flops 53214976 | bytes 2444288 | tf_op jit(solution)/shard_map/while/body/eval_jaxpr/qd,kd->qk/dot_general | solution.py:111
  420.4 24.0 %fusion.212 = (f32[256]{0:T(256)S(1)}, f32[256,1024]{1,0:T(8,128)S(1)}) fusion(f32[]{:T(128)} %bitcast.342, f32[]{:T(128)} %bitcast.343, f32[]{:T(128)} %bitcast.344, f32[]{:T(128)} %bitcast.345, f32[]{:T(128)} %bitcast.346, f32[]{:T(128)} %bitcast.347, f32[]{:T(128)} %bitcast.348, f32[]{:T(128)} %bitcast.349, f32[]{:T(128)} %bitcast.350, ...), kind=kOutput, calls=%fused_computation.211.clone.1 | convolution fusion | flops 53214976 | bytes 2444288 | tf_op jit(solution)/shard_map/while/body/eval_jaxpr/qd,kd->qk/dot_general | solution.py:111
  450.1 24.0 %fusion.212 = (f32[256]{0:T(256)S(1)}, f32[256,1024]{1,0:T(8,128)S(1)}) fusion(f32[]{:T(128)} %bitcast.342, f32[]{:T(128)} %bitcast.343, f32[]{:T(128)} %bitcast.344, f32[]{:T(128)} %bitcast.345, f32[]{:T(128)} %bitcast.346, f32[]{:T(128)} %bitcast.347, f32[]{:T(128)} %bitcast.348, f32[]{:T(128)} %bitcast.349, f32[]{:T(128)} %bitcast.350, ...), kind=kOutput, calls=%fused_computation.211.clone.1 | convolution fusion | flops 53214976 | bytes 2444288 | tf_op jit(solution)/shard_map/while/body/eval_jaxpr/qd,kd->qk/dot_general | solution.py:111
  503.6 82.5 %all-gather = bf16[32,24,4]{1,2,0:T(4,128)(2,1)S(1)} all-gather(bf16[1,24,4]{1,2,0:T(4,128)(2,1)S(1)} %bitcast.446), channel_id=1, replica_groups=mesh['dp'=2,'seq'=4,'expert'=4] {'dp','seq','expert'}, dimensions={0}, use_global_device_ids=true | all-gather | bytes 6336 | tf_op jit(solution)/shard_map/all_gather | solution.py:89
  706.1 471.3 %while.32 = (s32[]{:T(128)}, bf16[12,256,64]{1,2,0:T(8,128)(2,1)S(1)}, bf16[12,1024,64]{1,2,0:T(8,128)(2,1)S(1)}, bf16[12,1024,64]{1,2,0:T(8,128)(2,1)}, f32[12,...) while((s32[]{:T(128)}, ...), condition=%wide.region_20.22_spmd.clone.clone, body=%wide.region_18.21_spmd.clone.clone.sunk | while | flops 222641920 | bytes 16281661 | solution.py:279
  710.2 25.0 %multiply_reduce_fusion.8 = (f32[256]{0:T(256)S(1)}, f32[256,1024]{1,0:T(8,128)S(1)}) fusion(f32[256,1024]{1,0:T(8,128)S(1)} %fusion.225, f32[256]{0:T(256)S(1)} %bitcast.441, f32[]{:T(128)} %bitcast.390, f32[]{:T(128)} %bitcast.391, f32[]{:T(128)} %bitcast.392, f32[]{:T(128)} %bitcast.393, f32[]{:T(128)} %bitcast.394, f32[]{:T(128)} %bitcast.395, ...), kind=kOutput, calls=%fused_computation.48.clone.1 | convolution fusion | flops 53739264 | bytes 3493888 | tf_op jit(solution)/shard_map/while/body/eval_jaxpr/qd,kd->qk/dot_general | solution.py:111
  749.5 25.0 %multiply_reduce_fusion.8 = (f32[256]{0:T(256)S(1)}, f32[256,1024]{1,0:T(8,128)S(1)}) fusion(f32[256,1024]{1,0:T(8,128)S(1)} %fusion.225, f32[256]{0:T(256)S(1)} %bitcast.441, f32[]{:T(128)} %bitcast.390, f32[]{:T(128)} %bitcast.391, f32[]{:T(128)} %bitcast.392, f32[]{:T(128)} %bitcast.393, f32[]{:T(128)} %bitcast.394, f32[]{:T(128)} %bitcast.395, ...), kind=kOutput, calls=%fused_computation.48.clone.1 | convolution fusion | flops 53739264 | bytes 3493888 | tf_op jit(solution)/shard_map/while/body/eval_jaxpr/qd,kd->qk/dot_general | solution.py:111
  788.7 25.0 %multiply_reduce_fusion.8 = (f32[256]{0:T(256)S(1)}, f32[256,1024]{1,0:T(8,128)S(1)}) fusion(f32[256,1024]{1,0:T(8,128)S(1)} %fusion.225, f32[256]{0:T(256)S(1)} %bitcast.441, f32[]{:T(128)} %bitcast.390, f32[]{:T(128)} %bitcast.391, f32[]{:T(128)} %bitcast.392, f32[]{:T(128)} %bitcast.393, f32[]{:T(128)} %bitcast.394, f32[]{:T(128)} %bitcast.395, ...), kind=kOutput, calls=%fused_computation.48.clone.1 | convolution fusion | flops 53739264 | bytes 3493888 | tf_op jit(solution)/shard_map/while/body/eval_jaxpr/qd,kd->qk/dot_general | solution.py:111
  828.0 25.0 %multiply_reduce_fusion.8 = (f32[256]{0:T(256)S(1)}, f32[256,1024]{1,0:T(8,128)S(1)}) fusion(f32[256,1024]{1,0:T(8,128)S(1)} %fusion.225, f32[256]{0:T(256)S(1)} %bitcast.441, f32[]{:T(128)} %bitcast.390, f32[]{:T(128)} %bitcast.391, f32[]{:T(128)} %bitcast.392, f32[]{:T(128)} %bitcast.393, f32[]{:T(128)} %bitcast.394, f32[]{:T(128)} %bitcast.395, ...), kind=kOutput, calls=%fused_computation.48.clone.1 | convolution fusion | flops 53739264 | bytes 3493888 | tf_op jit(solution)/shard_map/while/body/eval_jaxpr/qd,kd->qk/dot_general | solution.py:111
  867.3 25.0 %multiply_reduce_fusion.8 = (f32[256]{0:T(256)S(1)}, f32[256,1024]{1,0:T(8,128)S(1)}) fusion(f32[256,1024]{1,0:T(8,128)S(1)} %fusion.225, f32[256]{0:T(256)S(1)} %bitcast.441, f32[]{:T(128)} %bitcast.390, f32[]{:T(128)} %bitcast.391, f32[]{:T(128)} %bitcast.392, f32[]{:T(128)} %bitcast.393, f32[]{:T(128)} %bitcast.394, f32[]{:T(128)} %bitcast.395, ...), kind=kOutput, calls=%fused_computation.48.clone.1 | convolution fusion | flops 53739264 | bytes 3493888 | tf_op jit(solution)/shard_map/while/body/eval_jaxpr/qd,kd->qk/dot_general | solution.py:111
  906.6 25.0 %multiply_reduce_fusion.8 = (f32[256]{0:T(256)S(1)}, f32[256,1024]{1,0:T(8,128)S(1)}) fusion(f32[256,1024]{1,0:T(8,128)S(1)} %fusion.225, f32[256]{0:T(256)S(1)} %bitcast.441, f32[]{:T(128)} %bitcast.390, f32[]{:T(128)} %bitcast.391, f32[]{:T(128)} %bitcast.392, f32[]{:T(128)} %bitcast.393, f32[]{:T(128)} %bitcast.394, f32[]{:T(128)} %bitcast.395, ...), kind=kOutput, calls=%fused_computation.48.clone.1 | convolution fusion | flops 53739264 | bytes 3493888 | tf_op jit(solution)/shard_map/while/body/eval_jaxpr/qd,kd->qk/dot_general | solution.py:111
  945.9 25.0 %multiply_reduce_fusion.8 = (f32[256]{0:T(256)S(1)}, f32[256,1024]{1,0:T(8,128)S(1)}) fusion(f32[256,1024]{1,0:T(8,128)S(1)} %fusion.225, f32[256]{0:T(256)S(1)} %bitcast.441, f32[]{:T(128)} %bitcast.390, f32[]{:T(128)} %bitcast.391, f32[]{:T(128)} %bitcast.392, f32[]{:T(128)} %bitcast.393, f32[]{:T(128)} %bitcast.394, f32[]{:T(128)} %bitcast.395, ...), kind=kOutput, calls=%fused_computation.48.clone.1 | convolution fusion | flops 53739264 | bytes 3493888 | tf_op jit(solution)/shard_map/while/body/eval_jaxpr/qd,kd->qk/dot_general | solution.py:111
  985.1 25.0 %multiply_reduce_fusion.8 = (f32[256]{0:T(256)S(1)}, f32[256,1024]{1,0:T(8,128)S(1)}) fusion(f32[256,1024]{1,0:T(8,128)S(1)} %fusion.225, f32[256]{0:T(256)S(1)} %bitcast.441, f32[]{:T(128)} %bitcast.390, f32[]{:T(128)} %bitcast.391, f32[]{:T(128)} %bitcast.392, f32[]{:T(128)} %bitcast.393, f32[]{:T(128)} %bitcast.394, f32[]{:T(128)} %bitcast.395, ...), kind=kOutput, calls=%fused_computation.48.clone.1 | convolution fusion | flops 53739264 | bytes 3493888 | tf_op jit(solution)/shard_map/while/body/eval_jaxpr/qd,kd->qk/dot_general | solution.py:111
  1024.4 25.0 %multiply_reduce_fusion.8 = (f32[256]{0:T(256)S(1)}, f32[256,1024]{1,0:T(8,128)S(1)}) fusion(f32[256,1024]{1,0:T(8,128)S(1)} %fusion.225, f32[256]{0:T(256)S(1)} %bitcast.441, f32[]{:T(128)} %bitcast.390, f32[]{:T(128)} %bitcast.391, f32[]{:T(128)} %bitcast.392, f32[]{:T(128)} %bitcast.393, f32[]{:T(128)} %bitcast.394, f32[]{:T(128)} %bitcast.395, ...), kind=kOutput, calls=%fused_computation.48.clone.1 | convolution fusion | flops 53739264 | bytes 3493888 | tf_op jit(solution)/shard_map/while/body/eval_jaxpr/qd,kd->qk/dot_general | solution.py:111
  1063.7 25.0 %multiply_reduce_fusion.8 = (f32[256]{0:T(256)S(1)}, f32[256,1024]{1,0:T(8,128)S(1)}) fusion(f32[256,1024]{1,0:T(8,128)S(1)} %fusion.225, f32[256]{0:T(256)S(1)} %bitcast.441, f32[]{:T(128)} %bitcast.390, f32[]{:T(128)} %bitcast.391, f32[]{:T(128)} %bitcast.392, f32[]{:T(128)} %bitcast.393, f32[]{:T(128)} %bitcast.394, f32[]{:T(128)} %bitcast.395, ...), kind=kOutput, calls=%fused_computation.48.clone.1 | convolution fusion | flops 53739264 | bytes 3493888 | tf_op jit(solution)/shard_map/while/body/eval_jaxpr/qd,kd->qk/dot_general | solution.py:111
  1103.0 25.0 %multiply_reduce_fusion.8 = (f32[256]{0:T(256)S(1)}, f32[256,1024]{1,0:T(8,128)S(1)}) fusion(f32[256,1024]{1,0:T(8,128)S(1)} %fusion.225, f32[256]{0:T(256)S(1)} %bitcast.441, f32[]{:T(128)} %bitcast.390, f32[]{:T(128)} %bitcast.391, f32[]{:T(128)} %bitcast.392, f32[]{:T(128)} %bitcast.393, f32[]{:T(128)} %bitcast.394, f32[]{:T(128)} %bitcast.395, ...), kind=kOutput, calls=%fused_computation.48.clone.1 | convolution fusion | flops 53739264 | bytes 3493888 | tf_op jit(solution)/shard_map/while/body/eval_jaxpr/qd,kd->qk/dot_general | solution.py:111
  1142.2 25.0 %multiply_reduce_fusion.8 = (f32[256]{0:T(256)S(1)}, f32[256,1024]{1,0:T(8,128)S(1)}) fusion(f32[256,1024]{1,0:T(8,128)S(1)} %fusion.225, f32[256]{0:T(256)S(1)} %bitcast.441, f32[]{:T(128)} %bitcast.390, f32[]{:T(128)} %bitcast.391, f32[]{:T(128)} %bitcast.392, f32[]{:T(128)} %bitcast.393, f32[]{:T(128)} %bitcast.394, f32[]{:T(128)} %bitcast.395, ...), kind=kOutput, calls=%fused_computation.48.clone.1 | convolution fusion | flops 53739264 | bytes 3493888 | tf_op jit(solution)/shard_map/while/body/eval_jaxpr/qd,kd->qk/dot_general | solution.py:111
  1229.6 40.4 %all-reduce.1 = (f32[768,4]{0,1:T(4,128)S(1)}, f32[2,768]{1,0:T(2,128)}, f32[32,12]{0,1:T(8,128)}) all-reduce(f32[768,4]{0,1:T(4,128)S(1)} %fusion.159, f32[2,768]{1,0:T(2,128)S(1)} %pad_maximum_fusion.5, f32[32,12]{0,1:T(8,128)S(1)} %bitcast.445), channel_id=5, replica_groups=mesh['dp'=2,'seq'=4,'expert'=4] {'dp','seq','expert'}, use_global_device_ids=true, to_apply=%region_25.27.clone | all-reduce | flops 4992 | bytes 39936
  1271.7 29.2 %reduce-scatter.12.cloned.1.call-done = bf16[96,6144]{1,0:T(8,128)(2,1)} async-done(((bf16[768,6144]{1,0:T(8,128)(2,1)}), bf16[96,6144]{1,0:T(8,128)(2,1)}) %reduce-scatter.12.cloned.1.call-update) | async-done | bytes 1179664 | tf_op jit(solution)/shard_map/reduce_scatter | solution.py:221
  1303.9 102.7 %reduce-scatter.10.cloned.1.call-done = f32[24,768]{1,0:T(8,128)} async-done(((f32[768,768]{1,0:T(8,128)}), f32[24,768]{1,0:T(8,128)}) %reduce-scatter.10.cloned.1.call-update) | async-done | bytes 73744 | tf_op jit(solution)/shard_map/reduce_scatter | solution.py:299
  1406.5 124.4 %reduce-scatter.8.cloned.1.call-done = f32[24,2304]{1,0:T(8,128)} async-done(((f32[768,2304]{1,0:T(8,128)}), f32[24,2304]{1,0:T(8,128)}) %reduce-scatter.8.cloned.1.call-update) | async-done | bytes 221200 | tf_op jit(solution)/shard_map/reduce_scatter | solution.py:298
  (437 shorter events, 491.4 us)
Async XLA Ops:
  7.2 66.6 %all-gather.7.cloned.1.call-start = ((), (), s32[]{:S(2)}) async-start(), calls=%async_computation.8 | async-start | bytes 3649536 | tf_op jit(solution)/shard_map/all_gather | solution.py:87
  7.9 97.6 %all-gather.9.cloned.1.call-start = ((), (), s32[]{:S(2)}) async-start(), calls=%async_computation.9 | async-start | bytes 3932160 | tf_op jit(solution)/shard_map/all_gather | solution.py:96
  8.7 69.3 %copy-start.16 = (f32[768]{0:T(1024)}, f32[768]{0:T(1024)S(1)}, u32[]{:S(2)}) copy-start(f32[768]{0:T(1024)S(1)} %get-tuple-element.297) | copy-start | bytes 9220
  9.9 68.1 %copy-start.25 = (f32[256]{0:T(256)}, f32[256]{0:T(256)S(1)}, u32[]{:S(2)}) copy-start(f32[256]{0:T(256)S(1)} %add_rsqrt_fusion.1) | copy-start | bytes 3076
  78.1 399.6 %all-gather.11.cloned.1.call-start = ((), (), s32[]{:S(2)}) async-start(), calls=%async_computation.10 | async-start | bytes 1216512 | tf_op jit(solution)/shard_map/all_gather | solution.py:88
  78.8 516.1 %all-gather.13.cloned.1.call-start = ((), (), s32[]{:S(2)}) async-start(), calls=%async_computation.11 | async-start | bytes 5308416 | tf_op jit(solution)/shard_map/all_gather | solution.py:158
  79.4 525.7 %all-gather.15.cloned.1.call-start = ((), (), s32[]{:S(2)}) async-start(), calls=%async_computation.12 | async-start | bytes 5308416 | tf_op jit(solution)/shard_map/all_gather | solution.py:159
  86.4 395.8 %copy-start.34 = (s32[512]{0:T(512)}, s32[512]{0:T(512)S(1)}, u32[]{:S(2)}) copy-start(s32[512]{0:T(512)S(1)} %multiply_add_fusion.1) | copy-start | bytes 6148
  121.1 358.2 %copy-start.1 = (bf16[1,256,768]{2,1,0:T(8,128)(2,1)S(1)}, bf16[1,256,768]{2,1,0:T(8,128)(2,1)}, u32[]{:S(2)}) copy-start(bf16[1,256,768]{2,1,0:T(8,128)(2,1)} %param.16) | copy-start | bytes 1179652
  481.5 104.8 %copy-start.2 = (bf16[256,768]{1,0:T(8,128)(2,1)}, bf16[256,768]{1,0:T(8,128)(2,1)S(1)}, u32[]{:S(2)}) copy-start(bf16[256,768]{1,0:T(8,128)(2,1)S(1)} %multiply_convert_fusion.4) | copy-start | bytes 1179652
  482.2 17.6 %copy-start.8 = (bf16[1,256,768]{2,1,0:T(8,128)(2,1)S(1)}, bf16[1,256,768]{2,1,0:T(8,128)(2,1)}, u32[]{:S(2)}) copy-start(bf16[1,256,768]{2,1,0:T(8,128)(2,1)} %param.25) | copy-start | bytes 1179652
  484.0 107.3 %all-to-all-start = ((bf16[4,192,768]{2,1,0:T(8,128)(2,1)}), bf16[4,192,768]{2,1,0:T(8,128)(2,1)}, u32[]{:S(2)}, u32[]{:S(2)}) async-start(bf16[4,192,768]{2,1,0:T(8,128)(2,1)} %bitcast.14), calls=%async_computation | async-start | bytes 2359296 | tf_op jit(solution)/shard_map/all_to_all | solution.py:149
  500.8 85.6 %copy-start.23 = (s32[1,256,2]{1,2,0:T(2,128)S(1)}, s32[1,256,2]{1,2,0:T(2,128)}, u32[]{:S(2)}) copy-start(s32[1,256,2]{1,2,0:T(2,128)} %param.24) | copy-start | bytes 6148
  500.8 87.1 %copy-start.35 = (s32[512]{0:T(512)S(1)}, s32[512]{0:T(512)}, u32[]{:S(2)}) copy-start(s32[512]{0:T(512)} %copy-done.34) | copy-start | bytes 6148
  587.7 17.4 %copy-start.36 = (f32[256,2]{0,1:T(2,128)}, f32[256,2]{0,1:T(2,128)S(1)}, u32[]{:S(2)}) copy-start(f32[256,2]{0,1:T(2,128)S(1)} %fusion.148) | copy-start | bytes 6148
  591.3 27.7 %all-to-all-start.2 = ((bf16[4,192,768]{2,1,0:T(8,128)(2,1)}), bf16[4,192,768]{2,1,0:T(8,128)(2,1)S(1)}, u32[]{:S(2)}, u32[]{:S(2)}) async-start(bf16[4,192,768]{2,1,0:T(8,128)(2,1)} %bitcast.438), calls=%async_computation.2 | async-start | bytes 2359296 | tf_op jit(solution)/shard_map/all_to_all | solution.py:186
  619.0 13.3 copy-start.41
  637.2 30.0 %all-to-all-start.3 = ((bf16[4,192,768]{2,1,0:T(8,128)(2,1)}), bf16[4,192,768]{2,1,0:T(8,128)(2,1)S(1)}, u32[]{:S(2)}, u32[]{:S(2)}) async-start(bf16[4,192,768]{2,1,0:T(8,128)(2,1)} %bitcast.439), calls=%async_computation.3 | async-start | bytes 2359296 | tf_op jit(solution)/shard_map/all_to_all | solution.py:206
  667.2 32.4 %all-to-all-start.1 = ((bf16[4,192,768]{2,1,0:T(8,128)(2,1)}), bf16[4,192,768]{2,1,0:T(8,128)(2,1)}, u32[]{:S(2)}, u32[]{:S(2)}) async-start(bf16[4,192,768]{2,1,0:T(8,128)(2,1)} %bitcast.437), calls=%async_computation.1 | async-start | bytes 2359296 | tf_op jit(solution)/shard_map/all_to_all | solution.py:166
  671.5 28.1 %copy-start.7 = (f32[256,768]{1,0:T(8,128)S(1)}, f32[256,768]{1,0:T(8,128)}, u32[]{:S(2)}) copy-start(f32[256,768]{1,0:T(8,128)} %copy-done.6) | copy-start | bytes 2359300
  671.5 548.2 %reduce-scatter.6.cloned.1.call-start = ((), (), s32[]{:S(2)}) async-start(), calls=%async_computation.13 | async-start | bytes 3932160 | tf_op jit(solution)/shard_map/reduce_scatter | solution.py:283
  677.1 25.0 %copy-start.21 = (f32[256]{0:T(256)S(1)}, f32[256]{0:T(256)}, u32[]{:S(2)}) copy-start(f32[256]{0:T(256)} %copy-done.20) | copy-start | bytes 3076
  677.1 25.0 %copy-start.30 = (f32[256]{0:T(256)S(1)}, f32[256]{0:T(256)}, u32[]{:S(2)}) copy-start(f32[256]{0:T(256)} %copy-done.29) | copy-start | bytes 3076
  677.1 25.1 %copy-start.24 = (s32[1,256,2]{1,2,0:T(2,128)S(1)}, s32[1,256,2]{1,2,0:T(2,128)}, u32[]{:S(2)}) copy-start(s32[1,256,2]{1,2,0:T(2,128)} %param.24) | copy-start | bytes 6148
  677.1 25.1 %copy-start.15 = (f32[256,768]{1,0:T(8,128)S(1)}, f32[256,768]{1,0:T(8,128)}, u32[]{:S(2)}) copy-start(f32[256,768]{1,0:T(8,128)} %convolution_reduce_fusion) | copy-start | bytes 2359300
  677.1 25.1 %copy-start.32 = (f32[256]{0:T(256)S(1)}, f32[256]{0:T(256)}, u32[]{:S(2)}) copy-start(f32[256]{0:T(256)} %copy-done.31) | copy-start | bytes 3076
  1180.8 120.1 %reduce-scatter.12.cloned.1.call-start = ((), (), s32[]{:S(2)}) async-start(), calls=%async_computation.16 | async-start | bytes 10616832 | tf_op jit(solution)/shard_map/reduce_scatter | solution.py:221
  1199.0 20.7 %copy-start.17 = (f32[768]{0:T(1024)S(1)}, f32[768]{0:T(1024)}, u32[]{:S(2)}) copy-start(f32[768]{0:T(1024)} %copy-done.16) | copy-start | bytes 9220
  1199.0 20.7 %copy-start.26 = (f32[256]{0:T(256)S(1)}, f32[256]{0:T(256)}, u32[]{:S(2)}) copy-start(f32[256]{0:T(256)} %copy-done.25) | copy-start | bytes 3076
  1199.0 207.6 %reduce-scatter.10.cloned.1.call-start = ((), (), s32[]{:S(2)}) async-start(), calls=%async_computation.15 | async-start | bytes 2433024 | tf_op jit(solution)/shard_map/reduce_scatter | solution.py:299
  1201.9 329.0 %reduce-scatter.8.cloned.1.call-start = ((), (), s32[]{:S(2)}) async-start(), calls=%async_computation.14 | async-start | bytes 7299072 | tf_op jit(solution)/shard_map/reduce_scatter | solution.py:298
  1226.2 44.4 %copy-start.27 = (f32[256]{0:T(256)S(1)}, f32[256]{0:T(256)}, u32[]{:S(2)}) copy-start(f32[256]{0:T(256)} %copy-done.25) | copy-start | bytes 3076
  (35 other events, 116.4 us)
Sparse Core Ops, SparseCore 0:
  10.9 62.8 all-gather.6
  78.2 27.3 all-gather.8
  108.5 54.1 all-gather.10
  164.4 37.8 all-gather.12
  204.0 38.9 all-gather.14
  1180.9 38.7 reduce-scatter.5
  1223.6 77.1 reduce-scatter.11
  1307.5 98.9 reduce-scatter.9
  1412.8 118.0 reduce-scatter.7
where the time goes:
time: 1550 us; the launch traced here: 1540 us
  matrix products  813 us (52%)
  waiting for transfers between devices  409 us (26%)
  local copies, waits for them, and re-layouts  124 us (8%)
  blocking collectives  123 us (8%)
  starting transfers between devices  28.1 us (2%)
  other arithmetic  24.6 us (2%)
    dot_general x24, matrix products, head_scores(): jnp.einsum('qd,kd->qk', queries_one, keys_one, preferred_element_type=jnp...  588 us
    reduce_scatter x1, waiting for transfers between devices, local(): lax.psum_scatter(qkv_part, ('dp', 'seq', 'expert'), scatter_dimension=0,...  124 us
    reduce_scatter x1, waiting for transfers between devices, local(): lax.psum_scatter(out_part, ('dp', 'seq', 'expert'), scatter_dimension=0,...  103 us
    all_gather x1, blocking collectives, local(): lax.all_gather(router_weight, ('dp', 'seq', 'expert'), axis=0, tiled=True)  82.5 us
    all_gather x1, waiting for transfers between devices, local(): lax.all_gather(qkv_weight, ('dp', 'seq', 'expert'), axis=0, tiled=True)  63.9 us
    dot_general x12, matrix products, head_backward(): jnp.einsum('qk,qkb->b', score_grad, bucket_onehot, preferred_element_type...  55.3 us
    unnamed x1, blocking collectives  40.4 us
    gather x48, local copies, waits for them, and re-layouts, head_scores(): raw_scores = raw_scores * score_scale + jnp.take(column, buckets)  34.1 us
  transfers between devices with their start and end apart: 13, of which 9 were waited for; matrix products, arithmetic and copies ran while one was open for 29% of the time, Pallas kernels for 0%

commit v1 on v0

v1 whole, which is shorter than its diff:
```python
import functools
import math

import jax
import jax.numpy as jnp
from jax import lax
from jax.experimental import pallas as pl
from jax.experimental.pallas import tpu as pltpu
from jax.sharding import PartitionSpec as P

D = 768
HEADS = 12
HEAD_DIM = 64
FF = 3072
BUCKETS = 32
LEN_DEV = 256


EPS = 1e-06
HIGH_PRECISION = lax.Precision.HIGHEST
CONTRACT_ROWS = (((0,), (0,)), ((), ()))


def bucket_edges(bucket_count):
    exact_count = bucket_count // 2
    boundaries = list(range(1, exact_count + 1))
    for bucket_index in range(exact_count + 1, bucket_count):
        power = (bucket_index - exact_count) / (bucket_count - exact_count)
        boundaries.append(math.ceil(exact_count * (128.0 / exact_count) ** power))
    return boundaries


def bucket_ids(distance, bucket_count):
    distance = jnp.maximum(distance, 0)
    bucket_sum = jnp.zeros(distance.shape, jnp.int32)
    for boundary in bucket_edges(bucket_count):
        bucket_sum = bucket_sum + (distance >= boundary).astype(jnp.int32)
    return bucket_sum


def norm_forward(values, scale_gain):
    inverse = lax.rsqrt(jnp.mean(values * values, axis=-1, keepdims=True) + EPS)
    normal_rows = values * inverse
    return (normal_rows * scale_gain, normal_rows, inverse)


def norm_backward(grad_out, normal_rows, inverse, scale_gain):
    gain_part = jnp.sum(grad_out * normal_rows, axis=0)
    scaled = grad_out * scale_gain
    value_grad = inverse * (
        scaled - normal_rows * jnp.mean(scaled * normal_rows, axis=-1, keepdims=True)
    )
    return (value_grad, gain_part)


def to_slots(slot_table, rows):
    return jnp.dot(slot_table, rows, preferred_element_type=jnp.float32).astype(jnp.bfloat16)


def from_slots(slot_table, rows):
    return lax.dot_general(slot_table, rows, CONTRACT_ROWS, preferred_element_type=jnp.float32)


TILE = 128
PAIR = 128
MASKED = -1e30
MATMUL_NT = (((1,), (1,)), ((), ()))


def matmul(left, right, dims=(((1,), (0,)), ((), ()))):
    return lax.dot_general(left, right, dims, preferred_element_type=jnp.float32)


def band_distance():
    key_row = lax.broadcasted_iota(jnp.int32, (2 * TILE, TILE), 0)
    query_column = lax.broadcasted_iota(jnp.int32, (2 * TILE, TILE), 1)
    return TILE + query_column - key_row


def fill_bias(strip, table_ref, head, tiles):
    distance = band_distance()
    band = jnp.full((2 * TILE, TILE), table_ref[0, head], jnp.float32)
    for bucket, edge in enumerate(bucket_edges(BUCKETS)):
        band = jnp.where(distance >= edge, table_ref[bucket + 1, head], band)
    band = jnp.where(distance >= 0, band, MASKED)
    far = (tiles - 2) * TILE
    strip[0:far, :] = jnp.full((far, TILE), table_ref[BUCKETS - 1, head], jnp.float32)
    strip[far : far + 2 * TILE, :] = band


def head_probabilities(strip, place, queries, keys, tiles):
    scores = matmul(keys, queries, MATMUL_NT)
    columns = []
    for part in range(LEN_DEV // TILE):
        start = (tiles - 1 - part) * TILE - place * LEN_DEV
        columns.append(strip[pl.ds(pl.multiple_of(start, TILE), tiles * TILE), :])
    scores = scores + jnp.concatenate(columns, axis=1)
    exps = jnp.exp(scores - jnp.max(scores, axis=0, keepdims=True))
    return exps * (1.0 / jnp.sum(exps, axis=0, keepdims=True))


def lane_halves(shape):
    return lax.broadcasted_iota(jnp.int32, shape, 1) < HEAD_DIM


def attend_kernel(tiles, place_ref, table_ref, q_ref, k_ref, v_ref, out_ref, strip):
    pair = pl.program_id(0)
    place = place_ref[0]

    @pl.when(pair == 0)
    def _():
        strip[tiles * TILE :, :] = jnp.full(((tiles - 1) * TILE, TILE), MASKED, jnp.float32)

    keys, values = k_ref[...], v_ref[...]
    queries = q_ref[...] * jnp.bfloat16(HEAD_DIM**-0.5)
    first = lane_halves(queries.shape)
    zero = jnp.zeros_like(queries)
    results = []
    for half in range(2):
        fill_bias(strip, table_ref, pair * 2 + half, tiles)
        own = jnp.where(first, queries, zero) if half == 0 else jnp.where(first, zero, queries)
        probs = head_probabilities(strip, place, own, keys, tiles).astype(jnp.bfloat16)
        results.append(matmul(values, probs, CONTRACT_ROWS))
    top = lax.broadcasted_iota(jnp.int32, results[0].shape, 0) < HEAD_DIM
    out_ref[...] = jnp.where(top, results[0], results[1]).T.astype(out_ref.dtype)


def attend_back_kernel(
    tiles, place_ref, table_ref, q_ref, k_ref, v_ref, g_ref, dq_ref, dkv_ref, sums_ref, strip, held
):
    pair = pl.program_id(0)
    place = place_ref[0]

    @pl.when(pair == 0)
    def _():
        strip[tiles * TILE :, :] = jnp.full(((tiles - 1) * TILE, TILE), MASKED, jnp.float32)

    keys, values = k_ref[...], v_ref[...]
    queries = q_ref[...] * jnp.bfloat16(HEAD_DIM**-0.5)
    grads = g_ref[...]
    first = lane_halves(queries.shape)
    zero = jnp.zeros_like(queries)
    distance = band_distance()
    buckets = jnp.full(distance.shape, -1, jnp.int32)
    for bucket, edge in enumerate([0] + bucket_edges(BUCKETS)):
        buckets = jnp.where(distance >= edge, bucket, buckets)
    q_parts, k_parts, v_parts = [], [], []
    for half in range(2):
        fill_bias(strip, table_ref, pair * 2 + half, tiles)
        own = jnp.where(first, queries, zero) if half == 0 else jnp.where(first, zero, queries)
        own_grads = jnp.where(first, grads, zero) if half == 0 else jnp.where(first, zero, grads)
        probs = head_probabilities(strip, place, own, keys, tiles)
        prob_grad = matmul(values, own_grads, MATMUL_NT)
        dots = jnp.sum(probs * prob_grad, axis=0, keepdims=True)
        score_grad = (probs * (prob_grad - dots)).astype(jnp.bfloat16)
        held[...] = score_grad
        k_parts.append(matmul(score_grad, queries))
        v_parts.append(matmul(probs.astype(jnp.bfloat16), grads))
        q_parts.append(matmul(keys, score_grad, CONTRACT_ROWS))
        band = jnp.zeros((2 * TILE, TILE), jnp.float32)
        for part in range(LEN_DEV // TILE):
            tile = place * (LEN_DEV // TILE) + part
            before = jnp.maximum(tile - 1, 0)
            cols = slice(part * TILE, (part + 1) * TILE)
            near = held[pl.ds(pl.multiple_of(before * TILE, TILE), TILE), cols].astype(jnp.float32)
            same = held[pl.ds(pl.multiple_of(tile * TILE, TILE), TILE), cols].astype(jnp.float32)
            near = jnp.where(tile > 0, near, 0.0)
            band = band + jnp.concatenate([near, same], axis=0)
        total = jnp.sum(score_grad.astype(jnp.float32), axis=0, keepdims=True)
        total = total[:, :TILE] + total[:, TILE:]
        far = total - jnp.sum(band, axis=0, keepdims=True)
        for bucket in range(BUCKETS):
            row = jnp.sum(jnp.where(buckets == bucket, band, 0.0), axis=0, keepdims=True)
            if bucket == BUCKETS - 1:
                row = row + far
            sums_ref[half, bucket : bucket + 1, :] = row
    top = lax.broadcasted_iota(jnp.int32, q_parts[0].shape, 0) < HEAD_DIM
    dq = jnp.where(top, q_parts[0], q_parts[1]).T * HEAD_DIM**-0.5
    dq_ref[...] = dq.astype(dq_ref.dtype)
    side = lane_halves(k_parts[0].shape)
    dkv_ref[0] = jnp.where(side, k_parts[0], k_parts[1]).astype(dkv_ref.dtype)
    dkv_ref[1] = jnp.where(side, v_parts[0], v_parts[1]).astype(dkv_ref.dtype)


def attention_specs(full_length):
    pairs = D // PAIR
    smem = pl.BlockSpec(memory_space=pltpu.SMEM)
    rows = pl.BlockSpec((LEN_DEV, PAIR), lambda pair: (0, pair))
    keys = pl.BlockSpec((full_length, PAIR), lambda pair: (0, pair))
    values = pl.BlockSpec((full_length, PAIR), lambda pair: (0, pair + pairs))
    return pairs, smem, rows, keys, values


def attend(place, bias_table, projected, key_values):
    full_length = key_values.shape[0]
    tiles = full_length // TILE
    pairs, smem, rows, keys, values = attention_specs(full_length)
    return pl.pallas_call(
        functools.partial(attend_kernel, tiles),
        grid=(pairs,),
        out_shape=jax.ShapeDtypeStruct((LEN_DEV, D), jnp.bfloat16),
        in_specs=[smem, smem, rows, keys, values],
        out_specs=rows,
        scratch_shapes=[pltpu.VMEM(((2 * tiles - 1) * TILE, TILE), jnp.float32)],
        compiler_params=pltpu.CompilerParams(vmem_limit_bytes=40 * 2**20),
        cost_estimate=pl.CostEstimate(
            flops=4 * LEN_DEV * full_length * PAIR * HEADS,
            bytes_accessed=2 * D * (2 * LEN_DEV + 2 * full_length),
            transcendentals=HEADS * LEN_DEV * full_length,
        ),
    )(place, bias_table, projected, key_values, key_values)


def attend_back(place, bias_table, projected, key_values, attended_grad):
    full_length = key_values.shape[0]
    tiles = full_length // TILE
    pairs, smem, rows, keys, values = attention_specs(full_length)
    return pl.pallas_call(
        functools.partial(attend_back_kernel, tiles),
        grid=(pairs,),
        out_shape=(
            jax.ShapeDtypeStruct((LEN_DEV, D), jnp.bfloat16),
            jax.ShapeDtypeStruct((2, full_length, D), jnp.bfloat16),
            jax.ShapeDtypeStruct((HEADS, BUCKETS, TILE), jnp.float32),
        ),
        in_specs=[smem, smem, rows, keys, values, rows],
        out_specs=(
            rows,
            pl.BlockSpec((2, full_length, PAIR), lambda pair: (0, 0, pair)),
            pl.BlockSpec((2, BUCKETS, TILE), lambda pair: (pair, 0, 0)),
        ),
        scratch_shapes=[
            pltpu.VMEM(((2 * tiles - 1) * TILE, TILE), jnp.float32),
            pltpu.VMEM((full_length, LEN_DEV), jnp.bfloat16),
        ],
        compiler_params=pltpu.CompilerParams(vmem_limit_bytes=48 * 2**20),
        cost_estimate=pl.CostEstimate(
            flops=10 * LEN_DEV * full_length * PAIR * HEADS,
            bytes_accessed=2 * D * (3 * LEN_DEV + 4 * full_length),
            transcendentals=HEADS * LEN_DEV * full_length,
        ),
    )(place, bias_table, projected, key_values, key_values, attended_grad)


def swap_experts(slots, experts_total):
    return lax.all_to_all(
        slots.reshape(experts_total, slots.shape[0] // experts_total, slots.shape[1]),
        "expert",
        split_axis=0,
        concat_axis=0,
        tiled=True,
    ).reshape(slots.shape)


def local(
    tokens,
    qkv_weight,
    out_weight,
    router_weight,
    w_in,
    w_out,
    norm_gains,
    bias_table,
    expert_ids,
    cotangent,
):
    everywhere = ("dp", "seq", "expert")
    inputs = tokens[0].astype(jnp.float32)
    experts_total = lax.axis_size("expert")
    capacity = 3 * LEN_DEV // experts_total
    router_pad = jnp.zeros((router_weight.shape[0], PAIR - experts_total), jnp.bfloat16)
    packed = jnp.concatenate([qkv_weight, out_weight, router_weight, router_pad], axis=1)
    packed = lax.all_gather(packed, everywhere, axis=0, tiled=True)
    qkv_full, out_full = packed[:, : 3 * D], packed[:, 3 * D : 4 * D]
    router_full = packed[:, 4 * D : 4 * D + experts_total]

    route_ids = expert_ids[0]
    expert_names = jnp.arange(experts_total, dtype=jnp.int32)
    choose = (route_ids[..., None] == expert_names).astype(jnp.float32)
    flat_ids = route_ids.reshape(-1)
    expert_hits = (flat_ids[:, None] == expert_names).astype(jnp.int32)
    slot_rank = jnp.sum((jnp.cumsum(expert_hits, axis=0) - 1) * expert_hits, axis=-1)
    places = (flat_ids * capacity + slot_rank).reshape(LEN_DEV, 2)
    slot_index = jnp.arange(experts_total * capacity, dtype=jnp.int32)[:, None]
    hits = [slot_index == places[None, :, k] for k in range(2)]
    tables = [hit.astype(jnp.bfloat16) for hit in hits]
    token_table = (hits[0] | hits[1]).astype(jnp.bfloat16)
    arrived_cotangent = swap_experts(to_slots(token_table, cotangent[0]), experts_total)

    normalized_rows, normal_one, inverse_one = norm_forward(inputs, norm_gains[0])
    normed_low = normalized_rows.astype(jnp.bfloat16)
    projected_rows = jnp.dot(normed_low, qkv_full, preferred_element_type=jnp.float32).astype(
        jnp.bfloat16
    )
    key_values = lax.all_gather(projected_rows[:, D:], "seq", axis=0, tiled=True)
    place = lax.axis_index("seq").astype(jnp.int32).reshape(1)
    attended_low = attend(place, bias_table, projected_rows, key_values)
    w_in_full = lax.all_gather(w_in, ("dp", "seq"), axis=1, tiled=True)[0]
    w_out_full = lax.all_gather(w_out, ("dp", "seq"), axis=2, tiled=True)[0]
    middle = inputs + jnp.dot(attended_low, out_full, preferred_element_type=jnp.float32)
    mixed, normal_two, inverse_two = norm_forward(middle, norm_gains[1])
    mixed_low = mixed.astype(jnp.bfloat16)
    expert_rows = swap_experts(to_slots(token_table, mixed_low), experts_total)
    router_logits = jnp.dot(mixed_low, router_full, preferred_element_type=jnp.float32)
    chosen = jnp.sum(choose * router_logits[:, None, :], axis=-1)
    gate_weights = jax.nn.softmax(chosen, axis=-1)
    gate_slots = jnp.sum(
        jnp.where(hits[0], gate_weights[None, :, 0], 0.0)
        + jnp.where(hits[1], gate_weights[None, :, 1], 0.0),
        axis=1,
    )
    arrived_gates = lax.all_to_all(
        gate_slots.reshape(experts_total, capacity),
        "expert",
        split_axis=0,
        concat_axis=0,
        tiled=True,
    ).reshape(-1, 1)
    pre_act = jnp.dot(expert_rows, w_in_full, preferred_element_type=jnp.float32)
    hidden_low = jax.nn.gelu(pre_act).astype(jnp.bfloat16)
    expert_out = jnp.dot(hidden_low, w_out_full, preferred_element_type=jnp.float32).astype(
        jnp.bfloat16
    )
    returned = swap_experts(expert_out, experts_total)
    arrived_grad = (arrived_gates * arrived_cotangent.astype(jnp.float32)).astype(jnp.bfloat16)
    hidden_grad = jnp.einsum(
        "rd,fd->rf", arrived_grad, w_out_full, preferred_element_type=jnp.float32
    )
    gelu_value, gelu_pull = jax.vjp(jax.nn.gelu, pre_act)
    pre_grad = gelu_pull(hidden_grad)[0].astype(jnp.bfloat16)
    row_grad = jnp.einsum(
        "rf,df->rd", pre_grad, w_in_full, preferred_element_type=jnp.float32
    ).astype(jnp.bfloat16)
    returned_grad = swap_experts(row_grad, experts_total)
    first_term = lax.dot_general(
        expert_rows, pre_grad, CONTRACT_ROWS, preferred_element_type=jnp.float32
    ).astype(jnp.bfloat16)
    second_term = lax.dot_general(
        arrived_grad, hidden_low, CONTRACT_ROWS, preferred_element_type=jnp.float32
    ).astype(jnp.bfloat16)

    upstream = cotangent[0].astype(jnp.float32)
    gathered = [from_slots(table, returned) for table in tables]
    block_out = middle + gate_weights[:, :1] * gathered[0] + gate_weights[:, 1:] * gathered[1]
    layer_out = block_out.astype(jnp.bfloat16)[None]
    gate_grad = jnp.stack([jnp.sum(upstream * rows, axis=-1) for rows in gathered], axis=-1)
    gate_mean = jnp.sum(gate_weights * gate_grad, axis=-1, keepdims=True)
    chosen_grad = gate_weights * (gate_grad - gate_mean)
    logit_grad = jnp.sum(choose * chosen_grad[..., None], axis=1)
    router_part = lax.dot_general(
        mixed_low.astype(jnp.float32), logit_grad, CONTRACT_ROWS, precision=HIGH_PRECISION
    )
    copy_back = from_slots(token_table, returned_grad)
    mixed_grad = copy_back + jnp.dot(
        logit_grad, router_full.astype(jnp.float32).T, precision=HIGH_PRECISION
    )
    middle_norm_grad, gain_two = norm_backward(mixed_grad, normal_two, inverse_two, norm_gains[1])
    middle_grad = upstream + middle_norm_grad
    branch_low = middle_grad.astype(jnp.bfloat16)
    attended_grad = jnp.einsum(
        "qe,de->qd", branch_low, out_full, preferred_element_type=jnp.float32
    ).astype(jnp.bfloat16)
    query_grad, kv_part, bucket_rows = attend_back(
        place, bias_table, projected_rows, key_values, attended_grad
    )
    kv_grad = lax.psum_scatter(kv_part, "seq", scatter_dimension=1, tiled=True)
    out_part = lax.dot_general(
        attended_low, branch_low, CONTRACT_ROWS, preferred_element_type=jnp.float32
    )
    expert_grad = lax.psum_scatter(
        jnp.concatenate([first_term, second_term], axis=1),
        ("dp", "seq"),
        scatter_dimension=0,
        tiled=True,
    ).astype(jnp.float32)
    w_in_grad = expert_grad[:, :FF][None]
    w_out_grad = expert_grad[:, FF:].T[None]
    projected_grad = jnp.concatenate([query_grad, kv_grad[0], kv_grad[1]], axis=1)
    qkv_part = lax.dot_general(
        normed_low, projected_grad, CONTRACT_ROWS, preferred_element_type=jnp.float32
    )
    router_part = jnp.pad(router_part, ((0, 0), (0, PAIR - experts_total)))
    weight_parts = jnp.concatenate([qkv_part, out_part, router_part], axis=1)
    weight_grads = lax.psum_scatter(
        weight_parts.astype(jnp.bfloat16), everywhere, scatter_dimension=0, tiled=True
    ).astype(jnp.float32)
    qkv_grad, out_grad = weight_grads[:, : 3 * D], weight_grads[:, 3 * D : 4 * D]
    router_grad = weight_grads[:, 4 * D : 4 * D + experts_total]
    normed_grad = jnp.einsum(
        "qe,de->qd", projected_grad, qkv_full, preferred_element_type=jnp.float32
    )
    input_norm_grad, gain_one = norm_backward(normed_grad, normal_one, inverse_one, norm_gains[0])
    input_grad = (middle_grad + input_norm_grad).astype(jnp.bfloat16)[None]
    gains_grad, table_grad = lax.psum(
        (jnp.stack([gain_one, gain_two]), jnp.sum(bucket_rows, axis=-1).T), everywhere
    )
    return (
        layer_out,
        input_grad,
        qkv_grad,
        out_grad,
        router_grad,
        w_in_grad,
        w_out_grad,
        gains_grad,
        table_grad,
    )


def solution(mesh):
    return jax.shard_map(
        local,
        mesh=mesh,
        in_specs=(
            P(("dp", "expert"), "seq", None),
            P(("dp", "seq", "expert"), None),
            P(("dp", "seq", "expert"), None),
            P(("dp", "seq", "expert"), None),
            P("expert", ("dp", "seq"), None),
            P("expert", None, ("dp", "seq")),
            P(),
            P(),
            P(("dp", "expert"), "seq", None),
            P(("dp", "expert"), "seq", None),
        ),
        out_specs=(
            P(("dp", "expert"), "seq", None),
            P(("dp", "expert"), "seq", None),
            P(("dp", "seq", "expert"), None),
            P(("dp", "seq", "expert"), None),
            P(("dp", "seq", "expert"), None),
            P("expert", ("dp", "seq"), None),
            P("expert", None, ("dp", "seq")),
            P(),
            P(),
        ),
        check_vma=False,
    )
```

time: 1550 us -> 608 us (0.39)
  matrix products: 813 us -> 79 us
  local copies, waits for them, and re-layouts: 124 us -> 22.3 us
  blocking collectives: 123 us -> 39.5 us
  Pallas kernels: 0 us -> 37.5 us
  waiting for transfers between devices: 409 us -> 372 us
    dot_general x103 -> x7, matrix products: 776 us -> 46.6 us  [the longest x1 13.4 us: local(): jnp.einsum('rd,fd->rf', arrived_grad, w_out_full, preferred_element_type=...]
    reduce_scatter x4 -> x2, waiting for transfers between devices: 274 us -> 43.9 us  [the longest x1 29.4 us: local(): lax.psum_scatter(jnp.concatenate([first_term, second_term], axis=1), ('dp...]
    unnamed x9 -> x8, waiting for transfers between devices: 2.5 us -> 109 us
    all_gather x1 -> x0, blocking collectives: 82.5 us -> none  [local(): lax.all_gather(router_weight, ('dp', 'seq', 'expert'), axis=0, tiled=True)]
    all_to_all x4 -> x5, waiting for transfers between devices: 51.2 us -> 94.8 us  [the longest x4 91.8 us: swap_experts(): lax.all_to_all(slots.reshape(experts_total, slots.shape[0] // experts_tot...]
    unnamed x1 -> x0, blocking collectives: 40.4 us -> none
    psum x0 -> x1, blocking collectives: none -> 39.5 us  [local(): lax.psum((jnp.stack([gain_one, gain_two]), jnp.sum(bucket_rows, axis=-1)....]
    pallas_call x0 -> x2, Pallas kernels: none -> 37.5 us  [the longest x1 23.2 us: attend_back(): pl.pallas_call(functools.partial(attend_back_kernel, tiles), grid=(pairs,...]
  transfers between devices with their start and end apart: 13 -> 12, of which waited for: 9 -> 12; matrix products, arithmetic and copies ran while one was open for 29% -> 10% of each run, Pallas kernels for 0% -> 2%
where the time goes in v1:
time: 608 us; the launch traced here: 607 us
  waiting for transfers between devices  372 us (61%)
  matrix products  79 us (13%)
  blocking collectives  39.5 us (6%)
  Pallas kernels  37.5 us (6%)
  local copies, waits for them, and re-layouts  22.3 us (4%)
  starting transfers between devices  21.1 us (3%)
  other arithmetic  20.8 us (3%)
  between operations  14.7 us (2%)
    unnamed x8, waiting for transfers between devices  109 us
    all_to_all x4, waiting for transfers between devices, swap_experts(): lax.all_to_all(slots.reshape(experts_total, slots.shape[0] // experts_tot...  91.8 us
    all_gather x1, waiting for transfers between devices, local(): packed = lax.all_gather(packed, everywhere, axis=0, tiled=True)  66.7 us
    psum x1, blocking collectives, local(): lax.psum((jnp.stack([gain_one, gain_two]), jnp.sum(bucket_rows, axis=-1)....  39.5 us
    reduce_scatter x1, waiting for transfers between devices, local(): lax.psum_scatter(jnp.concatenate([first_term, second_term], axis=1), ('dp...  29.4 us
    all_gather x1, waiting for transfers between devices, local(): lax.all_gather(projected_rows[:, D:], 'seq', axis=0, tiled=True)  23.5 us
    pallas_call x1, Pallas kernels, attend_back(): pl.pallas_call(functools.partial(attend_back_kernel, tiles), grid=(pairs,...  23.2 us
    all_gather x1, waiting for transfers between devices, local(): w_out_full = lax.all_gather(w_out, ('dp', 'seq'), axis=2, tiled=True)[0]  18.5 us
  transfers between devices with their start and end apart: 12, of which 12 were waited for; matrix products, arithmetic and copies ran while one was open for 10% of the time, Pallas kernels for 2%

profile of v1, /device:TPU:0, one launch (start us, length us, event | category | flops | bytes accessed | tf_op | source)
XLA Modules:
  0.0 606.7 jit_solution(11070971041834324377)
XLA Ops:
  11.7 66.7 %all-gather.5.cloned.1.call-done = bf16[768,3200]{1,0:T(8,128)(2,1)} async-done(((bf16[24,3200]{1,0:T(8,128)(2,1)}), bf16[768,3200]{1,0:T(8,128)(2,1)}) %all-gather.5.cloned.1.call-update) | async-done | bytes 4915216 | tf_op jit(solution)/shard_map/all_gather | solution.py:273
  78.5 3.3 convolution_convert_fusion.3.q_ref
  86.7 23.5 %all-gather.7.cloned.1.call-done.k_ref.v_ref = bf16[1024,1536]{1,0:T(8,128)(2,1)} async-done(((bf16[256,1536]{1,0:T(8,128)(2,1)}), bf16[1024,1536]{1,0:T(8,128)(2,1)}) %all-gather.7.cloned.1.call-update) | async-done | bytes 3145744 | tf_op jit(solution)/shard_map/all_gather | solution.py:295
  112.1 14.3 %shard_map.169 = bf16[256,768]{1,0:T(8,128)(2,1)S(1)} custom-call(s32[1]{0:T(128)} %bitcast.1.place_ref, f32[32,12]{1,0:T(8,128)S(1)} %copy.71.table_ref, bf16[256,2304]{1,0:T(8,128)(2,1)S(1)} %convolution_convert_fusion.3.q_ref, bf16[1024,1536]{1,0:T(8,128)(2,1)S(1)} %copy-done, bf16[1024,1536]{1,0:T(8,128)(2,1)S(1)} %copy-done), custom_call_target="tpu_custom_call" | custom-call | flops 1610612736 | bytes 3932160 | tf_op jit(solution)/shard_map/pallas_call | solution.py:198
  130.8 4.6 all-to-all-start
  135.4 15.6 %all-gather.9.cloned.1.call-done = bf16[1,768,3072]{2,1,0:T(8,128)(2,1)} async-done(((bf16[1,96,3072]{2,1,0:T(8,128)(2,1)}), bf16[1,768,3072]{2,1,0:T(8,128)(2,1)}) %all-gather.9.cloned.1.call-update) | async-done | bytes 4718608 | tf_op jit(solution)/shard_map/all_gather | solution.py:298
  151.1 13.3 %all-to-all-done = bf16[4,192,768]{2,1,0:T(8,128)(2,1)S(1)} async-done(((bf16[4,192,768]{2,1,0:T(8,128)(2,1)}), bf16[4,192,768]{2,1,0:T(8,128)(2,1)S(1)}, u32[]{:S(2)}, u32[]{:S(2)}) %all-to-all-start) | async-done | bytes 1179680 | tf_op jit(solution)/shard_map/all_to_all | solution.py:246
  164.4 8.9 %fusion.15 = f32[768,3072]{1,0:T(8,128)} fusion(bf16[768,768]{1,0:T(8,128)(2,1)S(1)} %bitcast.103, bf16[1,768,3072]{2,1,0:T(8,128)(2,1)} %all-gather.9.cloned.1.call-done), kind=kOutput, calls=%fused_computation.23 | convolution fusion | flops 3623878656 | bytes 15335424 | tf_op jit(solution)/shard_map/dot_general | solution.py:319
  173.3 18.5 %all-gather.11.cloned.1.call-done = bf16[1,3072,768]{1,2,0:T(8,128)(2,1)} async-done(((bf16[1,3072,96]{1,2,0:T(8,128)(2,1)}), bf16[1,3072,768]{1,2,0:T(8,128)(2,1)}) %all-gather.11.cloned.1.call-update) | async-done | bytes 4718608 | tf_op jit(solution)/shard_map/all_gather | solution.py:299
  191.7 11.7 %fusion.26 = bf16[768,768]{1,0:T(8,128)(2,1)} fusion(bf16[1,3072,768]{1,2,0:T(8,128)(2,1)} %all-gather.11.cloned.1.call-done, f32[768,3072]{1,0:T(8,128)} %fusion.15), kind=kOutput, calls=%fused_computation.33 | convolution fusion | flops 3645702144 | bytes 15335424 | tf_op jit(solution)/shard_map/dot_general | solution.py:321
  203.4 4.6 all-to-all-start.1
  210.0 27.0 %all-to-all-done.1 = bf16[4,192,768]{2,1,0:T(8,128)(2,1)S(1)} async-done(((bf16[4,192,768]{2,1,0:T(8,128)(2,1)}), bf16[4,192,768]{2,1,0:T(8,128)(2,1)S(1)}, u32[]{:S(2)}, u32[]{:S(2)}) %all-to-all-start.1) | async-done | bytes 1179680 | tf_op jit(solution)/shard_map/all_to_all | solution.py:246
  238.3 2.5 fusion.35
  243.0 3.2 all-to-all-start.2
  246.3 2.5 convolution_convert_fusion.5
  248.8 3.0 all-to-all-done.2
  252.4 3.7 all-to-all-start.3
  257.4 25.4 %all-to-all-done.3 = bf16[4,192,768]{2,1,0:T(8,128)(2,1)S(1)} async-done(((bf16[4,192,768]{2,1,0:T(8,128)(2,1)}), bf16[4,192,768]{2,1,0:T(8,128)(2,1)S(1)}, u32[]{:S(2)}, u32[]{:S(2)}) %all-to-all-start.3) | async-done | bytes 1179680 | tf_op jit(solution)/shard_map/all_to_all | solution.py:246
  284.0 13.4 %fusion.7 = bf16[768,3072]{1,0:T(8,128)(2,1)S(1)} fusion(f32[768,3072]{1,0:T(8,128)} %fusion.15, bf16[768,768]{1,0:T(8,128)(2,1)S(1)} %bitcast.109, bf16[1,3072,768]{1,2,0:T(8,128)(2,1)} %all-gather.11.cloned.1.call-done), kind=kOutput, calls=%fused_computation.10 | convolution fusion | flops 3671064576 | bytes 20054016 | tf_op jit(solution)/shard_map/rd,fd->rf/dot_general | solution.py:326
  297.5 4.9 fusion.23
  302.4 4.4 all-to-all-start.4
  308.9 26.0 %all-to-all-done.4 = bf16[4,192,768]{2,1,0:T(8,128)(2,1)} async-done(((bf16[4,192,768]{2,1,0:T(8,128)(2,1)}), bf16[4,192,768]{2,1,0:T(8,128)(2,1)}, u32[]{:S(2)}, u32[]{:S(2)}) %all-to-all-start.4) | async-done | bytes 1179680 | tf_op jit(solution)/shard_map/all_to_all | solution.py:246
  342.8 23.2 %shard_map.170 = (bf16[256,768]{1,0:T(8,128)(2,1)S(1)}, bf16[2,1024,768]{2,1,0:T(8,128)(2,1)S(1)}, f32[12,32,128]{2,1,0:T(8,128)S(1)}) custom-call(s32[1]{0:T(128)} %bitcast.1.place_ref, f32[32,12]{1,0:T(8,128)S(1)} %copy.71.table_ref, bf16[256,2304]{1,0:T(8,128)(2,1)S(1)} %convolution_convert_fusion.3.q_ref, ...), custom_call_target="tpu_custom_call" | custom-call | flops 4026531840 | bytes 7471104 | tf_op jit(solution)/shard_map/pallas_call | solution.py:218
  369.7 7.0 %convolution_convert_fusion.1 = bf16[768,3072]{1,0:T(8,128)(2,1)S(1)} fusion(bf16[768,768]{1,0:T(8,128)(2,1)S(1)} %bitcast.104, bf16[768,3072]{1,0:T(8,128)(2,1)} %copy-done.42), kind=kOutput, calls=%fused_computation.14 | convolution fusion | flops 3626237952 | bytes 10616832 | tf_op jit(solution)/shard_map/dot_general | solution.py:335
  376.7 6.8 %convolution_convert_fusion = bf16[768,3072]{1,0:T(8,128)(2,1)S(1)} fusion(bf16[768,768]{1,0:T(8,128)(2,1)S(1)} %fusion.20, f32[768,3072]{1,0:T(8,128)} %fusion.15), kind=kOutput, calls=%fused_computation.13 | convolution fusion | flops 3647471616 | bytes 15335424 | tf_op jit(solution)/shard_map/dot_general | solution.py:338
  383.6 4.0 pad_maximum_fusion
  389.5 14.5 %reduce-scatter.6.cloned.1.call-done = bf16[2,256,768]{2,1,0:T(8,128)(2,1)} async-done(((bf16[2,1024,768]{2,1,0:T(8,128)(2,1)}), bf16[2,256,768]{2,1,0:T(8,128)(2,1)}) %reduce-scatter.6.cloned.1.call-update) | async-done | bytes 786448 | tf_op jit(solution)/shard_map/reduce_scatter | solution.py:366
  407.8 2.6 fusion.8
  411.5 3.6 fusion.43
  415.1 39.5 %all-reduce.2 = (f32[2,768]{1,0:T(2,128)}, f32[32,12]{0,1:T(8,128)}) all-reduce(f32[2,768]{1,0:T(2,128)S(1)} %pad_maximum_fusion.4, f32[32,12]{0,1:T(8,128)S(1)} %bitcast.110), channel_id=1, replica_groups=mesh['dp'=2,'seq'=4,'expert'=4] {'dp','seq','expert'}, use_global_device_ids=true, to_apply=%region_20.21 | all-reduce | flops 1920 | bytes 15360 | tf_op jit(solution)/shard_map/psum | solution.py:394
  455.6 29.4 %reduce-scatter.8.cloned.1.call-done = bf16[96,6144]{1,0:T(8,128)(2,1)} async-done(((bf16[768,6144]{1,0:T(8,128)(2,1)}), bf16[96,6144]{1,0:T(8,128)(2,1)}) %reduce-scatter.8.cloned.1.call-update) | async-done | bytes 1179664 | tf_op jit(solution)/shard_map/reduce_scatter | solution.py:370
  488.0 107.5 %reduce-scatter.10.cloned.1.call-done = bf16[24,3200]{1,0:T(8,128)(2,1)} async-done(((bf16[768,3200]{1,0:T(8,128)(2,1)}), bf16[24,3200]{1,0:T(8,128)(2,1)}) %reduce-scatter.10.cloned.1.call-update) | async-done | bytes 153616
  (168 shorter events, 52.7 us)
Async XLA Ops:
  7.2 71.3 %all-gather.5.cloned.1.call-start = ((), (), s32[]{:S(2)}) async-start(), calls=%async_computation.8 | async-start | bytes 5068800 | tf_op jit(solution)/shard_map/all_gather | solution.py:273
  9.7 100.5 %all-gather.7.cloned.1.call-start = ((), (), s32[]{:S(2)}) async-start(), calls=%async_computation.9 | async-start | bytes 3932160 | tf_op jit(solution)/shard_map/all_gather | solution.py:295
  10.5 72.2 %copy-start.24 = (f32[768]{0:T(1024)}, f32[768]{0:T(1024)S(1)}, u32[]{:S(2)}) copy-start(f32[768]{0:T(1024)S(1)} %get-tuple-element.78) | copy-start | bytes 9220
  10.5 117.8 %copy-start.16 = (f32[768]{0:T(1024)}, f32[768]{0:T(1024)S(1)}, u32[]{:S(2)}) copy-start(f32[768]{0:T(1024)S(1)} %get-tuple-element.77) | copy-start | bytes 9220
  11.7 71.0 %copy-start.38 = (f32[256]{0:T(256)}, f32[256]{0:T(256)S(1)}, u32[]{:S(2)}) copy-start(f32[256]{0:T(256)S(1)} %add_rsqrt_fusion.1) | copy-start | bytes 3076
  82.7 68.3 %all-gather.9.cloned.1.call-start = ((), (), s32[]{:S(2)}) async-start(), calls=%async_computation.10 | async-start | bytes 5308416 | tf_op jit(solution)/shard_map/all_gather | solution.py:298
  83.5 108.3 %all-gather.11.cloned.1.call-start = ((), (), s32[]{:S(2)}) async-start(), calls=%async_computation.11 | async-start | bytes 5308416 | tf_op jit(solution)/shard_map/all_gather | solution.py:299
  84.0 42.4 %copy-start.10 = (bf16[1,256,768]{2,1,0:T(8,128)(2,1)S(1)}, bf16[1,256,768]{2,1,0:T(8,128)(2,1)}, u32[]{:S(2)}) copy-start(bf16[1,256,768]{2,1,0:T(8,128)(2,1)} %param.10) | copy-start | bytes 1179652
  86.7 42.6 %copy-start.29 = (s32[256]{0:T(256)}, s32[256]{0:T(256)S(1)}, u32[]{:S(2)}) copy-start(s32[256]{0:T(256)S(1)} %get-tuple-element.75) | copy-start | bytes 3076
  86.7 42.6 %copy-start.30 = (s32[256]{0:T(256)}, s32[256]{0:T(256)S(1)}, u32[]{:S(2)}) copy-start(s32[256]{0:T(256)S(1)} %get-tuple-element.76) | copy-start | bytes 3076
  129.3 78.8 %copy-start.6 = (bf16[256,768]{1,0:T(8,128)(2,1)}, bf16[256,768]{1,0:T(8,128)(2,1)S(1)}, u32[]{:S(2)}) copy-start(bf16[256,768]{1,0:T(8,128)(2,1)S(1)} %multiply_convert_fusion.2) | copy-start | bytes 1179652
  130.8 33.5 %all-to-all-start = ((bf16[4,192,768]{2,1,0:T(8,128)(2,1)}), bf16[4,192,768]{2,1,0:T(8,128)(2,1)S(1)}, u32[]{:S(2)}, u32[]{:S(2)}) async-start(bf16[4,192,768]{2,1,0:T(8,128)(2,1)} %bitcast.108), calls=%async_computation | async-start | bytes 2359296 | tf_op jit(solution)/shard_map/all_to_all | solution.py:246
  203.4 33.6 %all-to-all-start.1 = ((bf16[4,192,768]{2,1,0:T(8,128)(2,1)}), bf16[4,192,768]{2,1,0:T(8,128)(2,1)S(1)}, u32[]{:S(2)}, u32[]{:S(2)}) async-start(bf16[4,192,768]{2,1,0:T(8,128)(2,1)} %bitcast.106), calls=%async_computation.1 | async-start | bytes 2359296 | tf_op jit(solution)/shard_map/all_to_all | solution.py:246
  208.1 28.9 %copy-start.22 = (s32[256,2]{0,1:T(2,128)}, s32[256,2]{0,1:T(2,128)S(1)}, u32[]{:S(2)}) copy-start(s32[256,2]{0,1:T(2,128)S(1)} %copy.73) | copy-start | bytes 6148
  209.3 27.7 %copy-start.20 = (f32[256,2]{0,1:T(2,128)}, f32[256,2]{0,1:T(2,128)S(1)}, u32[]{:S(2)}) copy-start(f32[256,2]{0,1:T(2,128)S(1)} %select_reduce_fusion.1) | copy-start | bytes 6148
  209.4 27.6 %copy-start.35 = (f32[256]{0:T(256)}, f32[256]{0:T(256)S(1)}, u32[]{:S(2)}) copy-start(f32[256]{0:T(256)S(1)} %reduce_max.9) | copy-start | bytes 3076
  241.4 10.4 %copy-start.34 = (f32[256,1]{0,1:T(1,128)}, f32[256,1]{0,1:T(1,128)S(1)}, u32[]{:S(2)}) copy-start(f32[256,1]{0,1:T(1,128)S(1)} %get-tuple-element.90) | copy-start | bytes 3076
  243.0 8.8 %all-to-all-start.2 = ((f32[4,1,192]{2,1,0:T(1,128)}), f32[4,1,192]{2,1,0:T(1,128)S(1)}, u32[]{:S(2)}, u32[]{:S(2)}) async-start(f32[4,1,192]{2,1,0:T(1,128)} %all_to_all.20), calls=%async_computation.2 | async-start | bytes 8192 | tf_op jit(solution)/shard_map/all_to_all | solution.py:312
  252.4 30.5 %all-to-all-start.3 = ((bf16[4,192,768]{2,1,0:T(8,128)(2,1)}), bf16[4,192,768]{2,1,0:T(8,128)(2,1)S(1)}, u32[]{:S(2)}, u32[]{:S(2)}) async-start(bf16[4,192,768]{2,1,0:T(8,128)(2,1)} %bitcast.107), calls=%async_computation.3 | async-start | bytes 2359296 | tf_op jit(solution)/shard_map/all_to_all | solution.py:246
  282.9 14.6 %copy-start.2 = (bf16[4,192,768]{2,1,0:T(8,128)(2,1)}, bf16[4,192,768]{2,1,0:T(8,128)(2,1)S(1)}, u32[]{:S(2)}) copy-start(bf16[4,192,768]{2,1,0:T(8,128)(2,1)S(1)} %all-to-all-done.3) | copy-start | bytes 3538948
  282.9 14.6 %slice-start = ((s8[4718592]{0:T(1024)(128)(4,1)}), s8[4194304]{0:T(1024)(128)(4,1)S(1)}, s32[]{:S(2)}) async-start(s8[4718592]{0:T(1024)(128)(4,1)} %bitcast.121), calls=%async_computation.15 | async-start | bytes 8388608
  284.0 13.5 %slice-start.1 = ((s8[4718592]{0:T(1024)(128)(4,1)}), s8[524288]{0:T(1024)(128)(4,1)S(1)}, s32[]{:S(2)}) async-start(s8[4718592]{0:T(1024)(128)(4,1)} %bitcast.121), calls=%async_computation.16 | async-start | bytes 1048576
  302.4 34.5 %copy-start.4 = (f32[256,768]{1,0:T(8,128)S(1)}, f32[256,768]{1,0:T(8,128)}, u32[]{:S(2)}) copy-start(f32[256,768]{1,0:T(8,128)} %copy-done.3) | copy-start | bytes 2359300
  302.4 36.7 %copy-start.9 = (bf16[1,256,768]{2,1,0:T(8,128)(2,1)S(1)}, bf16[1,256,768]{2,1,0:T(8,128)(2,1)}, u32[]{:S(2)}) copy-start(bf16[1,256,768]{2,1,0:T(8,128)(2,1)} %param.19) | copy-start | bytes 1179652
  302.4 32.5 %all-to-all-start.4 = ((bf16[4,192,768]{2,1,0:T(8,128)(2,1)}), bf16[4,192,768]{2,1,0:T(8,128)(2,1)}, u32[]{:S(2)}, u32[]{:S(2)}) async-start(bf16[4,192,768]{2,1,0:T(8,128)(2,1)} %bitcast.105), calls=%async_computation.4 | async-start | bytes 2359296 | tf_op jit(solution)/shard_map/all_to_all | solution.py:246
  306.8 97.2 %reduce-scatter.6.cloned.1.call-start = ((), (), s32[]{:S(2)}) async-start(), calls=%async_computation.12 | async-start | bytes 3932160 | tf_op jit(solution)/shard_map/reduce_scatter | solution.py:366
  342.8 25.3 %copy-start.19 = (f32[4,1,192]{2,1,0:T(1,128)S(1)}, f32[4,1,192]{2,1,0:T(1,128)}, u32[]{:S(2)}) copy-start(f32[4,1,192]{2,1,0:T(1,128)} %copy-done.18) | copy-start | bytes 9220
  367.8 117.2 %reduce-scatter.8.cloned.1.call-start = ((), (), s32[]{:S(2)}) async-start(), calls=%async_computation.13 | async-start | bytes 10616832 | tf_op jit(solution)/shard_map/reduce_scatter | solution.py:370
  387.5 18.4 %copy-start.11 = (bf16[1,256,768]{2,1,0:T(8,128)(2,1)S(1)}, bf16[1,256,768]{2,1,0:T(8,128)(2,1)}, u32[]{:S(2)}) copy-start(bf16[1,256,768]{2,1,0:T(8,128)(2,1)} %param.10) | copy-start | bytes 1179652
  387.5 18.4 %copy-start.25 = (f32[768]{0:T(1024)S(1)}, f32[768]{0:T(1024)}, u32[]{:S(2)}) copy-start(f32[768]{0:T(1024)} %copy-done.24) | copy-start | bytes 9220
  387.6 208.0 %reduce-scatter.10.cloned.1.call-start = ((), (), s32[]{:S(2)}) async-start(), calls=%async_computation.14 | async-start | bytes 5068800
  411.5 43.1 %copy-start.26 = (f32[768]{0:T(1024)S(1)}, f32[768]{0:T(1024)}, u32[]{:S(2)}) copy-start(f32[768]{0:T(1024)} %copy-done.24) | copy-start | bytes 9220
  (25 other events, 73.6 us)
Sparse Core Ops, SparseCore 0:
  11.4 66.9 all-gather.4
  82.8 27.3 all-gather.6
  112.1 38.9 all-gather.8
  152.8 38.9 all-gather.10
  367.9 36.0 reduce-scatter.5
  407.8 77.1 reduce-scatter.7
  491.6 103.8 reduce-scatter.9

commit v2 on v1

--- a/solution.py
+++ b/solution.py
@@ -92,8 +92,12 @@
     scores = matmul(keys, queries, MATMUL_NT)
     columns = []
     for part in range(LEN_DEV // TILE):
-        start = (tiles - 1 - part) * TILE - place * LEN_DEV
-        columns.append(strip[pl.ds(pl.multiple_of(start, TILE), tiles * TILE), :])
+        blocks = []
+        for slot in range(tiles * TILE // LEN_DEV):
+            owner = jnp.bitwise_xor(place, slot)
+            start = (tiles - 1 - part) * TILE + (owner - place) * LEN_DEV
+            blocks.append(strip[pl.ds(pl.multiple_of(start, TILE), LEN_DEV), :])
+        columns.append(jnp.concatenate(blocks, axis=0))
     scores = scores + jnp.concatenate(columns, axis=1)
     exps = jnp.exp(scores - jnp.max(scores, axis=0, keepdims=True))
     return exps * (1.0 / jnp.sum(exps, axis=0, keepdims=True))
@@ -159,12 +163,15 @@
         q_parts.append(matmul(keys, score_grad, CONTRACT_ROWS))
         band = jnp.zeros((2 * TILE, TILE), jnp.float32)
         for part in range(LEN_DEV // TILE):
-            tile = place * (LEN_DEV // TILE) + part
-            before = jnp.maximum(tile - 1, 0)
             cols = slice(part * TILE, (part + 1) * TILE)
-            near = held[pl.ds(pl.multiple_of(before * TILE, TILE), TILE), cols].astype(jnp.float32)
-            same = held[pl.ds(pl.multiple_of(tile * TILE, TILE), TILE), cols].astype(jnp.float32)
-            near = jnp.where(tile > 0, near, 0.0)
+            same = score_grad[part * TILE : (part + 1) * TILE, cols].astype(jnp.float32)
+            if part > 0:
+                near = score_grad[(part - 1) * TILE : part * TILE, cols].astype(jnp.float32)
+            else:
+                slot = jnp.bitwise_xor(place, jnp.maximum(place - 1, 0))
+                start = (slot + 1) * LEN_DEV - TILE
+                near = held[pl.ds(pl.multiple_of(start, TILE), TILE), cols].astype(jnp.float32)
+                near = jnp.where(place > 0, near, 0.0)
             band = band + jnp.concatenate([near, same], axis=0)
         total = jnp.sum(score_grad.astype(jnp.float32), axis=0, keepdims=True)
         total = total[:, :TILE] + total[:, TILE:]
@@ -178,8 +185,10 @@
     dq = jnp.where(top, q_parts[0], q_parts[1]).T * HEAD_DIM**-0.5
     dq_ref[...] = dq.astype(dq_ref.dtype)
     side = lane_halves(k_parts[0].shape)
-    dkv_ref[0] = jnp.where(side, k_parts[0], k_parts[1]).astype(dkv_ref.dtype)
-    dkv_ref[1] = jnp.where(side, v_parts[0], v_parts[1]).astype(dkv_ref.dtype)
+    for index, parts in enumerate((k_parts, v_parts)):
+        both = jnp.where(side, parts[0], parts[1]).astype(dkv_ref.dtype)
+        for slot in range(dkv_ref.shape[0]):
+            dkv_ref[slot, index] = both[slot * LEN_DEV : (slot + 1) * LEN_DEV]
 
 
 def attention_specs(full_length):
@@ -220,13 +229,15 @@
         grid=(pairs,),
         out_shape=(
             jax.ShapeDtypeStruct((LEN_DEV, D), jnp.bfloat16),
-            jax.ShapeDtypeStruct((2, full_length, D), jnp.bfloat16),
+            jax.ShapeDtypeStruct((full_length // LEN_DEV, 2, LEN_DEV, D), jnp.bfloat16),
             jax.ShapeDtypeStruct((HEADS, BUCKETS, TILE), jnp.float32),
         ),
         in_specs=[smem, smem, rows, keys, values, rows],
         out_specs=(
             rows,
-            pl.BlockSpec((2, full_length, PAIR), lambda pair: (0, 0, pair)),
+            pl.BlockSpec(
+                (full_length // LEN_DEV, 2, LEN_DEV, PAIR), lambda pair: (0, 0, 0, pair)
+            ),
             pl.BlockSpec((2, BUCKETS, TILE), lambda pair: (pair, 0, 0)),
         ),
         scratch_shapes=[
@@ -240,6 +251,34 @@
             transcendentals=HEADS * LEN_DEV * full_length,
         ),
     )(place, bias_table, projected, key_values, key_values, attended_grad)
+
+
+def swap_pairs(block, bit):
+    pairs = [(index, index ^ bit) for index in range(lax.axis_size("seq"))]
+    return lax.ppermute(block, "seq", pairs)
+
+
+def spread_sequence(block):
+    held = {0: block}
+    bit = lax.axis_size("seq") // 2
+    while bit:
+        held.update({slot ^ bit: swap_pairs(held[slot], bit) for slot in list(held)})
+        bit //= 2
+    return [held[slot] for slot in range(len(held))]
+
+
+def sum_sequence(parts):
+    held = {slot: parts[slot] for slot in range(parts.shape[0])}
+    bit = 1
+    while bit < parts.shape[0]:
+        kept = {}
+        for slot in held:
+            if not slot & bit:
+                arrived = swap_pairs(held[slot ^ bit].astype(jnp.bfloat16), bit)
+                kept[slot] = held[slot].astype(jnp.float32) + arrived.astype(jnp.float32)
+        held = kept
+        bit *= 2
+    return held[0].astype(jnp.bfloat16)
 
 
 def swap_experts(slots, experts_total):
@@ -270,7 +309,8 @@
     capacity = 3 * LEN_DEV // experts_total
     router_pad = jnp.zeros((router_weight.shape[0], PAIR - experts_total), jnp.bfloat16)
     packed = jnp.concatenate([qkv_weight, out_weight, router_weight, router_pad], axis=1)
-    packed = lax.all_gather(packed, everywhere, axis=0, tiled=True)
+    packed = lax.all_gather(packed, "expert", axis=0, tiled=True)
+    packed = lax.all_gather(packed, ("dp", "seq"), axis=0, tiled=True)
     qkv_full, out_full = packed[:, : 3 * D], packed[:, 3 * D : 4 * D]
     router_full = packed[:, 4 * D : 4 * D + experts_total]
 
@@ -289,10 +329,11 @@
 
     normalized_rows, normal_one, inverse_one = norm_forward(inputs, norm_gains[0])
     normed_low = normalized_rows.astype(jnp.bfloat16)
+    normed_low, arrived_cotangent = lax.optimization_barrier((normed_low, arrived_cotangent))
     projected_rows = jnp.dot(normed_low, qkv_full, preferred_element_type=jnp.float32).astype(
         jnp.bfloat16
     )
-    key_values = lax.all_gather(projected_rows[:, D:], "seq", axis=0, tiled=True)
+    key_values = jnp.concatenate(spread_sequence(projected_rows[:, D:]), axis=0)
     place = lax.axis_index("seq").astype(jnp.int32).reshape(1)
     attended_low = attend(place, bias_table, projected_rows, key_values)
     w_in_full = lax.all_gather(w_in, ("dp", "seq"), axis=1, tiled=True)[0]
@@ -339,6 +380,9 @@
         arrived_grad, hidden_low, CONTRACT_ROWS, preferred_element_type=jnp.float32
     ).astype(jnp.bfloat16)
 
+    returned, first_term, second_term = lax.optimization_barrier(
+        (returned, first_term, second_term)
+    )
     upstream = cotangent[0].astype(jnp.float32)
     gathered = [from_slots(table, returned) for table in tables]
     block_out = middle + gate_weights[:, :1] * gathered[0] + gate_weights[:, 1:] * gathered[1]
@@ -363,26 +407,30 @@
     query_grad, kv_part, bucket_rows = attend_back(
         place, bias_table, projected_rows, key_values, attended_grad
     )
-    kv_grad = lax.psum_scatter(kv_part, "seq", scatter_dimension=1, tiled=True)
+    kv_grad = sum_sequence(kv_part)
     out_part = lax.dot_general(
         attended_low, branch_low, CONTRACT_ROWS, preferred_element_type=jnp.float32
     )
-    expert_grad = lax.psum_scatter(
-        jnp.concatenate([first_term, second_term], axis=1),
-        ("dp", "seq"),
-        scatter_dimension=0,
-        tiled=True,
-    ).astype(jnp.float32)
-    w_in_grad = expert_grad[:, :FF][None]
-    w_out_grad = expert_grad[:, FF:].T[None]
+    first_sum, second_sum = [
+        lax.psum_scatter(term, ("dp", "seq"), scatter_dimension=0, tiled=True)
+        for term in (first_term, second_term)
+    ]
     projected_grad = jnp.concatenate([query_grad, kv_grad[0], kv_grad[1]], axis=1)
+    projected_grad, first_sum, second_sum = lax.optimization_barrier(
+        (projected_grad, first_sum, second_sum)
+    )
+    w_in_grad = first_sum.astype(jnp.float32)[None]
+    w_out_grad = second_sum.astype(jnp.float32).T[None]
     qkv_part = lax.dot_general(
         normed_low, projected_grad, CONTRACT_ROWS, preferred_element_type=jnp.float32
     )
     router_part = jnp.pad(router_part, ((0, 0), (0, PAIR - experts_total)))
     weight_parts = jnp.concatenate([qkv_part, out_part, router_part], axis=1)
     weight_grads = lax.psum_scatter(
-        weight_parts.astype(jnp.bfloat16), everywhere, scatter_dimension=0, tiled=True
+        weight_parts.astype(jnp.bfloat16), ("dp", "seq"), scatter_dimension=0, tiled=True
+    )
+    weight_grads = lax.psum_scatter(
+        weight_grads, "expert", scatter_dimension=0, tiled=True
     ).astype(jnp.float32)
     qkv_grad, out_grad = weight_grads[:, : 3 * D], weight_grads[:, 3 * D : 4 * D]
     router_grad = weight_grads[:, 4 * D : 4 * D + experts_total]

time: 608 us -> 451 us (0.74)
  waiting for transfers between devices: 372 us -> 188 us
  blocking collectives: 39.5 us -> 58.3 us
  other arithmetic: 20.8 us -> 13.6 us
    all_gather x2 -> x1, waiting for transfers between devices: 90.2 us -> 4.43 us  [local(): packed = lax.all_gather(packed, ('dp', 'seq'), axis=0, tiled=True)]
    unnamed x8, waiting for transfers between devices: 109 us -> 23 us
    ppermute x0 -> x6, waiting for transfers between devices: none -> 57.9 us  [swap_pairs(): return lax.ppermute(block, 'seq', pairs)]
    reduce_scatter x2 -> x3, waiting for transfers between devices: 43.9 us -> 22.5 us  [the longest x2 11.3 us: local(): lax.psum_scatter(term, ('dp', 'seq'), scatter_dimension=0, tiled=True)]
    all_gather x0 -> x1, blocking collectives: none -> 18.7 us  [local(): packed = lax.all_gather(packed, 'expert', axis=0, tiled=True)]
    all_gather x1, waiting for transfers between devices: 18.5 us -> 0.01 us  [local(): w_out_full = lax.all_gather(w_out, ('dp', 'seq'), axis=2, tiled=True)[0]]
    all_gather x1, waiting for transfers between devices: 15.6 us -> 0.01 us  [local(): w_in_full = lax.all_gather(w_in, ('dp', 'seq'), axis=1, tiled=True)[0]]
    all_to_all x4, waiting for transfers between devices: 91.8 us -> 76.6 us  [swap_experts(): lax.all_to_all(slots.reshape(experts_total, slots.shape[0] // experts_tot...]
  transfers between devices with their start and end apart: 12 -> 18, of which waited for: 12 -> 12; matrix products, arithmetic and copies ran while one was open for 10% -> 20% of each run, Pallas kernels for 2% -> 9%
where the time goes in v2:
time: 451 us; the launch traced here: 444 us
  waiting for transfers between devices  188 us (42%)
  matrix products  84.5 us (19%)
  blocking collectives  58.3 us (13%)
  Pallas kernels  38.6 us (9%)
  starting transfers between devices  26.4 us (6%)
  local copies, waits for them, and re-layouts  19.2 us (4%)
  between operations  15.2 us (3%)
  other arithmetic  13.6 us (3%)
    all_to_all x4, waiting for transfers between devices, swap_experts(): lax.all_to_all(slots.reshape(experts_total, slots.shape[0] // experts_tot...  76.6 us
    ppermute x6, waiting for transfers between devices, swap_pairs(): return lax.ppermute(block, 'seq', pairs)  57.9 us
    psum x1, blocking collectives, local(): lax.psum((jnp.stack([gain_one, gain_two]), jnp.sum(bucket_rows, axis=-1)....  39.6 us
    pallas_call x1, Pallas kernels, attend_back(): pl.pallas_call(functools.partial(attend_back_kernel, tiles), grid=(pairs,...  24.1 us
    unnamed x8, waiting for transfers between devices  23 us
    all_gather x1, blocking collectives, local(): packed = lax.all_gather(packed, 'expert', axis=0, tiled=True)  18.7 us
    all_to_all x4, starting transfers between devices, swap_experts(): lax.all_to_all(slots.reshape(experts_total, slots.shape[0] // experts_tot...  18.2 us
    pallas_call x1, Pallas kernels, attend(): pl.pallas_call(functools.partial(attend_kernel, tiles), grid=(pairs,), ou...  14.5 us
  transfers between devices with their start and end apart: 18, of which 12 were waited for; matrix products, arithmetic and copies ran while one was open for 20% of the time, Pallas kernels for 9%

profile of v2, /device:TPU:0, one launch (start us, length us, event | category | flops | bytes accessed | tf_op | source)
XLA Modules:
  0.0 444.2 jit_solution(14059279353103495097)
XLA Ops:
  9.1 18.7 %all_gather.12 = bf16[96,3200]{1,0:T(8,128)(2,1)} all-gather(bf16[24,3200]{1,0:T(8,128)(2,1)S(1)} %concatenate.17), channel_id=1, replica_groups=mesh['dp'=2,'seq'=4,'expert'=4] {'expert'}, dimensions={0}, use_global_device_ids=true | all-gather | bytes 768000 | tf_op jit(solution)/shard_map/all_gather | solution.py:312
  34.3 5.2 %all-to-all-start = ((bf16[4,192,768]{2,1,0:T(8,128)(2,1)}), bf16[4,192,768]{2,1,0:T(8,128)(2,1)S(1)}, u32[]{:S(2)}, u32[]{:S(2)}) async-start(bf16[4,192,768]{2,1,0:T(8,128)(2,1)} %bitcast.6), calls=%async_computation | async-start | bytes 2359296 | tf_op jit(solution)/shard_map/all_to_all | solution.py:285
  41.2 23.6 %all-to-all-done = bf16[4,192,768]{2,1,0:T(8,128)(2,1)S(1)} async-done(((bf16[4,192,768]{2,1,0:T(8,128)(2,1)}), bf16[4,192,768]{2,1,0:T(8,128)(2,1)S(1)}, u32[]{:S(2)}, u32[]{:S(2)}) %all-to-all-start) | async-done | bytes 1179680 | tf_op jit(solution)/shard_map/all_to_all | solution.py:285
  64.8 4.4 all-gather.4.cloned.1.call-done
  69.3 3.1 convolution_convert_fusion.3.q_ref
  74.8 24.7 %collective-permute-done.1 = bf16[256,1536]{1,0:T(8,128)(2,1)S(1)} collective-permute-done((bf16[256,1536]{1,0:T(8,128)(2,1)S(1)}, bf16[256,1536]{1,0:T(8,128)(2,1)S(1)}, u32[]{:S(2)}, u32[]{:S(2)}) %collective-permute-start.1) | collective-permute-done | bytes 786464 | tf_op jit(solution)/shard_map/ppermute | solution.py:258
  100.2 2.8 collective-permute-done.2
  104.6 14.5 %shard_map.169 = bf16[256,768]{1,0:T(8,128)(2,1)S(1)} custom-call(s32[1]{0:T(128)} %bitcast.1.place_ref, f32[32,12]{1,0:T(8,128)S(1)} %copy.74.table_ref, bf16[256,2304]{1,0:T(8,128)(2,1)S(1)} %copy-done.2, bf16[1024,1536]{1,0:T(8,128)(2,1)S(1)} %pad_maximum_fusion.k_ref.v_ref, bf16[1024,1536]{1,0:T(8,128)(2,1)S(1)} %pad_maximum_fusion.k_ref.v_ref), custom_call_target="tpu_custom_call" | custom-call | flops 1610612736 | bytes 3932160 | tf_op jit(solution)/shard_map/pallas_call | solution.py:207
  124.3 4.6 %all-to-all-start.3 = ((f32[4,1,192]{2,1,0:T(1,128)}), f32[4,1,192]{2,1,0:T(1,128)S(1)}, u32[]{:S(2)}, u32[]{:S(2)}) async-start(f32[4,1,192]{2,1,0:T(1,128)} %all_to_all.21), calls=%async_computation.3 | async-start | bytes 8192 | tf_op jit(solution)/shard_map/all_to_all | solution.py:353
  130.4 4.1 all-to-all-done.3
  134.5 4.5 %all-to-all-start.1 = ((bf16[4,192,768]{2,1,0:T(8,128)(2,1)}), bf16[4,192,768]{2,1,0:T(8,128)(2,1)}, u32[]{:S(2)}, u32[]{:S(2)}) async-start(bf16[4,192,768]{2,1,0:T(8,128)(2,1)} %bitcast.9), calls=%async_computation.1 | async-start | bytes 2359296 | tf_op jit(solution)/shard_map/all_to_all | solution.py:285
  139.1 27.6 %all-to-all-done.1 = bf16[4,192,768]{2,1,0:T(8,128)(2,1)} async-done(((bf16[4,192,768]{2,1,0:T(8,128)(2,1)}), bf16[4,192,768]{2,1,0:T(8,128)(2,1)}, u32[]{:S(2)}, u32[]{:S(2)}) %all-to-all-start.1) | async-done | bytes 1179680 | tf_op jit(solution)/shard_map/all_to_all | solution.py:285
  166.7 10.2 %fusion.15 = f32[768,3072]{1,0:T(8,128)} fusion(bf16[768,768]{1,0:T(8,128)(2,1)} %bitcast.10, bf16[1,768,3072]{2,1,0:T(8,128)(2,1)} %all-gather.6.cloned.1.call-done), kind=kOutput, calls=%fused_computation.22 | convolution fusion | flops 3623878656 | bytes 15335424 | tf_op jit(solution)/shard_map/dot_general | solution.py:360
  176.9 11.7 %fusion.28 = bf16[768,768]{1,0:T(8,128)(2,1)} fusion(bf16[1,3072,768]{1,2,0:T(8,128)(2,1)} %all-gather.8.cloned.1.call-done, f32[768,3072]{1,0:T(8,128)} %fusion.15), kind=kOutput, calls=%fused_computation.36 | convolution fusion | flops 3645702144 | bytes 15335424 | tf_op jit(solution)/shard_map/dot_general | solution.py:362
  188.5 3.5 all-to-all-start.2
  192.3 13.0 %fusion.7 = bf16[768,3072]{1,0:T(8,128)(2,1)S(1)} fusion(f32[768,3072]{1,0:T(8,128)} %fusion.15, bf16[1,3072,768]{1,2,0:T(8,128)(2,1)} %all-gather.8.cloned.1.call-done, bf16[768,768]{1,0:T(8,128)(2,1)S(1)} %bitcast.108, f32[768]{0:T(1024)S(1)} %mul.234), kind=kOutput, calls=%fused_computation.10 | convolution fusion | flops 3672834048 | bytes 20057088 | tf_op jit(solution)/shard_map/rd,fd->rf/dot_general | solution.py:367
  207.4 7.0 %convolution_convert_fusion.2 = bf16[768,3072]{1,0:T(8,128)(2,1)} fusion(bf16[768,768]{1,0:T(8,128)(2,1)} %bitcast.10, bf16[768,3072]{1,0:T(8,128)(2,1)S(1)} %fusion.7), kind=kOutput, calls=%fused_computation.14 | convolution fusion | flops 3626237952 | bytes 10616832 | tf_op jit(solution)/shard_map/dot_general | solution.py:376
  214.4 8.5 %convolution_convert_fusion.1 = bf16[768,3072]{1,0:T(8,128)(2,1)} fusion(bf16[768,768]{1,0:T(8,128)(2,1)S(1)} %bitcast.109, f32[768]{0:T(1024)S(1)} %mul.234, f32[768,3072]{1,0:T(8,128)} %fusion.15), kind=kOutput, calls=%fused_computation.13 | convolution fusion | flops 3649241088 | bytes 15338496 | tf_op jit(solution)/shard_map/dot_general | solution.py:379
  223.5 8.7 %fusion.25 = bf16[768,768]{1,0:T(8,128)(2,1)} fusion(bf16[768,3072]{1,0:T(8,128)(2,1)} %copy-done.36, bf16[1,768,3072]{2,1,0:T(8,128)(2,1)} %all-gather.6.cloned.1.call-done), kind=kOutput, calls=%fused_computation.35 | convolution fusion | flops 3624468480 | bytes 10616832 | tf_op jit(solution)/shard_map/rf,df->rd/dot_general | solution.py:372
  232.3 5.0 %all-to-all-start.4 = ((bf16[4,192,768]{2,1,0:T(8,128)(2,1)}), bf16[4,192,768]{2,1,0:T(8,128)(2,1)}, u32[]{:S(2)}, u32[]{:S(2)}) async-start(bf16[4,192,768]{2,1,0:T(8,128)(2,1)} %bitcast.110), calls=%async_computation.4 | async-start | bytes 2359296 | tf_op jit(solution)/shard_map/all_to_all | solution.py:285
  239.6 25.3 %all-to-all-done.4 = bf16[4,192,768]{2,1,0:T(8,128)(2,1)} async-done(((bf16[4,192,768]{2,1,0:T(8,128)(2,1)}), bf16[4,192,768]{2,1,0:T(8,128)(2,1)}, u32[]{:S(2)}, u32[]{:S(2)}) %all-to-all-start.4) | async-done | bytes 1179680 | tf_op jit(solution)/shard_map/all_to_all | solution.py:285
  272.0 24.1 %shard_map.170 = (bf16[256,768]{1,0:T(8,128)(2,1)S(1)}, bf16[4,2,256,768]{3,2,1,0:T(8,128)(2,1)S(1)}, f32[12,32,128]{2,1,0:T(8,128)S(1)}) custom-call(s32[1]{0:T(128)} %bitcast.1.place_ref, f32[32,12]{1,0:T(8,128)S(1)} %copy.74.table_ref, bf16[256,2304]{1,0:T(8,128)(2,1)S(1)} %copy-done.3, bf16[1024,1536]{1,0:T(8,128)(2,1)} %copy-done, ...), custom_call_target="tpu_custom_call" | custom-call | flops 4026531840 | bytes 7471104 | tf_op jit(solution)/shard_map/pallas_call | solution.py:227
  299.0 2.9 collective-permute-done.4
  305.2 2.7 convolution_convert_fusion.4
  307.9 27.5 %collective-permute-done.5 = bf16[2,256,768]{2,1,0:T(8,128)(2,1)} collective-permute-done((bf16[2,256,768]{2,1,0:T(8,128)(2,1)}, bf16[2,256,768]{2,1,0:T(8,128)(2,1)}, u32[]{:S(2)}, u32[]{:S(2)}) %collective-permute-start.5) | collective-permute-done | bytes 786464 | tf_op jit(solution)/shard_map/ppermute | solution.py:258
  337.3 11.3 %reduce-scatter.9.cloned.1.call-done = bf16[96,3072]{1,0:T(8,128)(2,1)} async-done(((bf16[768,3072]{1,0:T(8,128)(2,1)}), bf16[96,3072]{1,0:T(8,128)(2,1)}) %reduce-scatter.9.cloned.1.call-update) | async-done | bytes 589840 | tf_op jit(solution)/shard_map/reduce_scatter | solution.py:415
  349.8 2.6 fusion.8
  353.5 3.3 fusion.45
  356.8 39.6 %all-reduce.2 = (f32[2,768]{1,0:T(2,128)}, f32[32,12]{0,1:T(8,128)}) all-reduce(f32[2,768]{1,0:T(2,128)S(1)} %pad_maximum_fusion.2, f32[32,12]{0,1:T(8,128)S(1)} %bitcast.112), channel_id=1, replica_groups=mesh['dp'=2,'seq'=4,'expert'=4] {'dp','seq','expert'}, use_global_device_ids=true, to_apply=%region_21.22 | all-reduce | flops 1920 | bytes 15360 | tf_op jit(solution)/shard_map/psum | solution.py:442
  396.5 11.2 %reduce-scatter.11.cloned.1.call-done = bf16[96,3200]{1,0:T(8,128)(2,1)} async-done(((bf16[768,3200]{1,0:T(8,128)(2,1)}), bf16[96,3200]{1,0:T(8,128)(2,1)}) %reduce-scatter.11.cloned.1.call-update) | async-done | bytes 614416 | tf_op jit(solution)/shard_map/reduce_scatter | solution.py:429
  408.7 2.9 convert_bitcast_fusion
  411.6 21.0 %reduce-scatter.13.cloned.1.call-done = bf16[24,3200]{1,0:T(8,128)(2,1)} async-done(((bf16[96,3200]{1,0:T(8,128)(2,1)}), bf16[24,3200]{1,0:T(8,128)(2,1)}) %reduce-scatter.13.cloned.1.call-update) | async-done | bytes 153616
  (166 shorter events, 49.3 us)
Async XLA Ops:
  7.2 33.0 %copy-start.35 = (f32[2,768]{1,0:T(2,128)S(1)}, f32[2,768]{1,0:T(2,128)}, u32[]{:S(2)}) copy-start(f32[2,768]{1,0:T(2,128)} %param.16) | copy-start | bytes 18436
  7.2 33.6 %copy-start.15 = (bf16[1,256,768]{2,1,0:T(8,128)(2,1)S(1)}, bf16[1,256,768]{2,1,0:T(8,128)(2,1)}, u32[]{:S(2)}) copy-start(bf16[1,256,768]{2,1,0:T(8,128)(2,1)} %param.10) | copy-start | bytes 1179652
  7.2 62.1 %all-gather.4.cloned.1.call-start = ((), (), s32[]{:S(2)}) async-start(), calls=%async_computation.9 | async-start | bytes 5529600 | tf_op jit(solution)/shard_map/all_gather | solution.py:313
  27.8 111.3 %all-gather.6.cloned.1.call-start = ((), (), s32[]{:S(2)}) async-start(), calls=%async_computation.10 | async-start | bytes 5308416 | tf_op jit(solution)/shard_map/all_gather | solution.py:339
  31.8 40.6 %copy-start.28 = (s32[256]{0:T(256)}, s32[256]{0:T(256)S(1)}, u32[]{:S(2)}) copy-start(s32[256]{0:T(256)S(1)} %get-tuple-element.92) | copy-start | bytes 3076
  31.8 40.6 %copy-start.32 = (s32[256]{0:T(256)}, s32[256]{0:T(256)S(1)}, u32[]{:S(2)}) copy-start(s32[256]{0:T(256)S(1)} %get-tuple-element.91) | copy-start | bytes 3076
  34.3 30.6 %all-to-all-start = ((bf16[4,192,768]{2,1,0:T(8,128)(2,1)}), bf16[4,192,768]{2,1,0:T(8,128)(2,1)S(1)}, u32[]{:S(2)}, u32[]{:S(2)}) async-start(bf16[4,192,768]{2,1,0:T(8,128)(2,1)} %bitcast.6), calls=%async_computation | async-start | bytes 2359296 | tf_op jit(solution)/shard_map/all_to_all | solution.py:285
  39.5 137.4 %all-gather.8.cloned.1.call-start = ((), (), s32[]{:S(2)}) async-start(), calls=%async_computation.11 | async-start | bytes 5308416 | tf_op jit(solution)/shard_map/all_gather | solution.py:340
  40.8 31.6 %copy-start.22 = (f32[768]{0:T(1024)}, f32[768]{0:T(1024)S(1)}, u32[]{:S(2)}) copy-start(f32[768]{0:T(1024)S(1)} %get-tuple-element.94) | copy-start | bytes 9220
  40.8 58.7 %copy-start.34 = (f32[32,12]{0,1:T(8,128)S(1)}, f32[32,12]{0,1:T(8,128)}, u32[]{:S(2)}) copy-start(f32[32,12]{0,1:T(8,128)} %param.17) | copy-start | bytes 4612
  41.0 63.5 %copy-start.30 = (f32[256]{0:T(256)}, f32[256]{0:T(256)S(1)}, u32[]{:S(2)}) copy-start(f32[256]{0:T(256)S(1)} %add_rsqrt_fusion.1) | copy-start | bytes 3076
  41.2 28.1 %copy-start.17 = (bf16[256,768]{1,0:T(8,128)(2,1)}, bf16[256,768]{1,0:T(8,128)(2,1)S(1)}, u32[]{:S(2)}) copy-start(bf16[256,768]{1,0:T(8,128)(2,1)S(1)} %fusion.39) | copy-start | bytes 1179652
  73.5 26.0 %collective-permute-start.1 = (bf16[256,1536]{1,0:T(8,128)(2,1)S(1)}, bf16[256,1536]{1,0:T(8,128)(2,1)S(1)}, u32[]{:S(2)}, u32[]{:S(2)}) collective-permute-start(bf16[256,1536]{1,0:T(8,128)(2,1)S(1)} %slice.92), channel_id=1, source_target_pairs={{0,8},{4,12},{8,0},{12,4},{1,9},{5,13},{9,1},{13,5},{2,10},{6,14},... | collective-permute-start | bytes 2359304 | tf_op jit(solution)/shard_map/ppermute | solution.py:258
  74.8 25.5 %collective-permute-start = (bf16[256,1536]{1,0:T(8,128)(2,1)S(1)}, bf16[256,1536]{1,0:T(8,128)(2,1)}, u32[]{:S(2)}, u32[]{:S(2)}) collective-permute-start(bf16[256,1536]{1,0:T(8,128)(2,1)S(1)} %slice.92), channel_id=1, source_target_pairs={{0,4},{4,0},{8,12},{12,8},{1,5},{5,1},{9,13},{13,9},{2,6},{6,2},{1... | collective-permute-start | bytes 2359304 | tf_op jit(solution)/shard_map/ppermute | solution.py:258
  99.5 3.5 collective-permute-start.2
  104.6 18.8 %copy-start.29 = (s32[256]{0:T(256)S(1)}, s32[256]{0:T(256)}, u32[]{:S(2)}) copy-start(s32[256]{0:T(256)} %copy-done.28) | copy-start | bytes 3076
  122.0 54.9 %copy-start.13 = (bf16[256,768]{1,0:T(8,128)(2,1)}, bf16[256,768]{1,0:T(8,128)(2,1)S(1)}, u32[]{:S(2)}) copy-start(bf16[256,768]{1,0:T(8,128)(2,1)S(1)} %multiply_convert_fusion.2) | copy-start | bytes 1179652
  124.3 10.2 %all-to-all-start.3 = ((f32[4,1,192]{2,1,0:T(1,128)}), f32[4,1,192]{2,1,0:T(1,128)S(1)}, u32[]{:S(2)}, u32[]{:S(2)}) async-start(f32[4,1,192]{2,1,0:T(1,128)} %all_to_all.21), calls=%async_computation.3 | async-start | bytes 8192 | tf_op jit(solution)/shard_map/all_to_all | solution.py:353
  134.5 32.2 %all-to-all-start.1 = ((bf16[4,192,768]{2,1,0:T(8,128)(2,1)}), bf16[4,192,768]{2,1,0:T(8,128)(2,1)}, u32[]{:S(2)}, u32[]{:S(2)}) async-start(bf16[4,192,768]{2,1,0:T(8,128)(2,1)} %bitcast.9), calls=%async_computation.1 | async-start | bytes 2359296 | tf_op jit(solution)/shard_map/all_to_all | solution.py:285
  188.5 34.4 %all-to-all-start.2 = ((bf16[4,192,768]{2,1,0:T(8,128)(2,1)}), bf16[4,192,768]{2,1,0:T(8,128)(2,1)S(1)}, u32[]{:S(2)}, u32[]{:S(2)}) async-start(bf16[4,192,768]{2,1,0:T(8,128)(2,1)} %bitcast.111), calls=%async_computation.2 | async-start | bytes 2359296 | tf_op jit(solution)/shard_map/all_to_all | solution.py:285
  192.1 145.2 %reduce-scatter.7.cloned.1.call-start = ((), (), s32[]{:S(2)}) async-start(), calls=%async_computation.12 | async-start | bytes 5308416 | tf_op jit(solution)/shard_map/reduce_scatter | solution.py:415
  222.9 125.7 %reduce-scatter.9.cloned.1.call-start = ((), (), s32[]{:S(2)}) async-start(), calls=%async_computation.13 | async-start | bytes 5308416 | tf_op jit(solution)/shard_map/reduce_scatter | solution.py:415
  232.3 32.6 %all-to-all-start.4 = ((bf16[4,192,768]{2,1,0:T(8,128)(2,1)}), bf16[4,192,768]{2,1,0:T(8,128)(2,1)}, u32[]{:S(2)}, u32[]{:S(2)}) async-start(bf16[4,192,768]{2,1,0:T(8,128)(2,1)} %bitcast.110), calls=%async_computation.4 | async-start | bytes 2359296 | tf_op jit(solution)/shard_map/all_to_all | solution.py:285
  237.3 170.3 %reduce-scatter.11.cloned.1.call-start = ((), (), s32[]{:S(2)}) async-start(), calls=%async_computation.14 | async-start | bytes 5529600 | tf_op jit(solution)/shard_map/reduce_scatter | solution.py:429
  239.6 29.7 %copy-start.24 = (f32[256,4]{0,1:T(4,128)}, f32[256,4]{0,1:T(4,128)S(1)}, u32[]{:S(2)}) copy-start(f32[256,4]{0,1:T(4,128)S(1)} %select_reduce_fusion) | copy-start | bytes 12292
  298.5 3.4 collective-permute-start.4
  298.5 9.5 %collective-permute-start.3 = (bf16[2,256,768]{2,1,0:T(8,128)(2,1)}, bf16[2,256,768]{2,1,0:T(8,128)(2,1)}, u32[]{:S(2)}, u32[]{:S(2)}) collective-permute-start(bf16[2,256,768]{2,1,0:T(8,128)(2,1)} %get-tuple-element.97), channel_id=1, source_target_pairs={{0,4},{4,0},{8,12},{12,8},{1,5},{5,1},{9,13},{13,9},{2,6},{6,2},{1... | collective-permute-start | bytes 2359304 | tf_op jit(solution)/shard_map/ppermute | solution.py:258
  302.9 32.5 %collective-permute-start.5 = (bf16[2,256,768]{2,1,0:T(8,128)(2,1)}, bf16[2,256,768]{2,1,0:T(8,128)(2,1)}, u32[]{:S(2)}, u32[]{:S(2)}) collective-permute-start(bf16[2,256,768]{2,1,0:T(8,128)(2,1)} %fusion.22), channel_id=1, source_target_pairs={{0,8},{4,12},{8,0},{12,4},{1,9},{5,13},{9,1},{13,5},{2,10},{6,14},... | collective-permute-start | bytes 2359304 | tf_op jit(solution)/shard_map/ppermute | solution.py:258
  305.2 32.0 %copy-start.5 = (bf16[256,768]{1,0:T(8,128)(2,1)S(1)}, bf16[256,768]{1,0:T(8,128)(2,1)}, u32[]{:S(2)}) copy-start(bf16[256,768]{1,0:T(8,128)(2,1)} %copy-done.4) | copy-start | bytes 1179652
  307.9 40.7 %copy-start.18 = (bf16[256,768]{1,0:T(8,128)(2,1)S(1)}, bf16[256,768]{1,0:T(8,128)(2,1)}, u32[]{:S(2)}) copy-start(bf16[256,768]{1,0:T(8,128)(2,1)} %copy-done.17) | copy-start | bytes 1179652
  352.4 80.2 %reduce-scatter.13.cloned.1.call-start = ((), (), s32[]{:S(2)}) async-start(), calls=%async_computation.15 | async-start | bytes 768000
  353.5 54.2 %copy-start.11 = (f32[256,768]{1,0:T(8,128)S(1)}, f32[256,768]{1,0:T(8,128)}, u32[]{:S(2)}) copy-start(f32[256,768]{1,0:T(8,128)} %copy-done.10) | copy-start | bytes 2359300
  (23 other events, 161.3 us)
Sparse Core Ops, SparseCore 0:
  27.9 41.3 all-gather.3
  71.1 45.3 all-gather.5
  118.4 38.9 all-gather.7
  223.1 54.2 reduce-scatter.6
  281.1 67.4 reduce-scatter.8
  352.5 55.0 reduce-scatter.10
  410.0 22.5 reduce-scatter.12

commit v3 on v2

--- a/solution.py
+++ b/solution.py
@@ -350,6 +350,7 @@
         + jnp.where(hits[1], gate_weights[None, :, 1], 0.0),
         axis=1,
     )
+    gate_slots, expert_rows = lax.optimization_barrier((gate_slots, expert_rows))
     arrived_gates = lax.all_to_all(
         gate_slots.reshape(experts_total, capacity),
         "expert",
@@ -372,6 +373,7 @@
     row_grad = jnp.einsum(
         "rf,df->rd", pre_grad, w_in_full, preferred_element_type=jnp.float32
     ).astype(jnp.bfloat16)
+    row_grad, pre_grad, hidden_low = lax.optimization_barrier((row_grad, pre_grad, hidden_low))
     returned_grad = swap_experts(row_grad, experts_total)
     first_term = lax.dot_general(
         expert_rows, pre_grad, CONTRACT_ROWS, preferred_element_type=jnp.float32
@@ -380,9 +382,8 @@
         arrived_grad, hidden_low, CONTRACT_ROWS, preferred_element_type=jnp.float32
     ).astype(jnp.bfloat16)
 
-    returned, first_term, second_term = lax.optimization_barrier(
-        (returned, first_term, second_term)
-    )
+    expert_terms = jnp.concatenate([first_term, second_term], axis=1)
+    returned, expert_terms = lax.optimization_barrier((returned, expert_terms))
     upstream = cotangent[0].astype(jnp.float32)
     gathered = [from_slots(table, returned) for table in tables]
     block_out = middle + gate_weights[:, :1] * gathered[0] + gate_weights[:, 1:] * gathered[1]
@@ -411,16 +412,13 @@
     out_part = lax.dot_general(
         attended_low, branch_low, CONTRACT_ROWS, preferred_element_type=jnp.float32
     )
-    first_sum, second_sum = [
-        lax.psum_scatter(term, ("dp", "seq"), scatter_dimension=0, tiled=True)
-        for term in (first_term, second_term)
-    ]
+    expert_grad = lax.psum_scatter(
+        expert_terms, ("dp", "seq"), scatter_dimension=0, tiled=True
+    )
     projected_grad = jnp.concatenate([query_grad, kv_grad[0], kv_grad[1]], axis=1)
-    projected_grad, first_sum, second_sum = lax.optimization_barrier(
-        (projected_grad, first_sum, second_sum)
-    )
-    w_in_grad = first_sum.astype(jnp.float32)[None]
-    w_out_grad = second_sum.astype(jnp.float32).T[None]
+    projected_grad, expert_grad = lax.optimization_barrier((projected_grad, expert_grad))
+    w_in_grad = expert_grad[:, :FF].astype(jnp.float32)[None]
+    w_out_grad = expert_grad[:, FF:].astype(jnp.float32).T[None]
     qkv_part = lax.dot_general(
         normed_low, projected_grad, CONTRACT_ROWS, preferred_element_type=jnp.float32
     )

time: 451 us -> 413 us (0.916); the launches traced: 444 us -> 412 us
  waiting for transfers between devices: 188 us -> 161 us
  matrix products: 84.5 us -> 78.6 us
  other arithmetic: 13.6 us -> 18.4 us
    reduce_scatter x2 -> x1, waiting for transfers between devices: 11.3 us -> 0.02 us  [local(): lax.psum_scatter(expert_terms, ('dp', 'seq'), scatter_dimension=0, tiled=...]
    ppermute x6, waiting for transfers between devices: 57.9 us -> 48.3 us  [swap_pairs(): return lax.ppermute(block, 'seq', pairs)]
    unnamed x79 -> x67, local copies, waits for them, and re-layouts: 10.5 us -> 8.43 us
    unnamed x8 -> x7, waiting for transfers between devices: 23 us -> 21.7 us
  transfers between devices with their start and end apart: 18 -> 17, of which waited for: 12 -> 10; matrix products, arithmetic and copies ran while one was open for 20% -> 23% of each run, Pallas kernels for 9% -> 9%
where the time goes in v3:
time: 413 us; the launch traced here: 412 us
  waiting for transfers between devices  161 us (39%)
  matrix products  78.6 us (19%)
  blocking collectives  58.3 us (14%)
  Pallas kernels  38.6 us (9%)
  starting transfers between devices  26.4 us (6%)
  other arithmetic  18.4 us (4%)
  local copies, waits for them, and re-layouts  16 us (4%)
  between operations  14.6 us (4%)
    all_to_all x4, waiting for transfers between devices, swap_experts(): lax.all_to_all(slots.reshape(experts_total, slots.shape[0] // experts_tot...  77.2 us
    ppermute x6, waiting for transfers between devices, swap_pairs(): return lax.ppermute(block, 'seq', pairs)  48.3 us
    psum x1, blocking collectives, local(): lax.psum((jnp.stack([gain_one, gain_two]), jnp.sum(bucket_rows, axis=-1)....  39.6 us
    pallas_call x1, Pallas kernels, attend_back(): pl.pallas_call(functools.partial(attend_back_kernel, tiles), grid=(pairs,...  24.1 us
    unnamed x7, waiting for transfers between devices  21.7 us
    all_to_all x4, starting transfers between devices, swap_experts(): lax.all_to_all(slots.reshape(experts_total, slots.shape[0] // experts_tot...  19.9 us
    all_gather x1, blocking collectives, local(): packed = lax.all_gather(packed, 'expert', axis=0, tiled=True)  18.7 us
    pallas_call x1, Pallas kernels, attend(): pl.pallas_call(functools.partial(attend_kernel, tiles), grid=(pairs,), ou...  14.5 us
  transfers between devices with their start and end apart: 17, of which 10 were waited for; matrix products, arithmetic and copies ran while one was open for 23% of the time, Pallas kernels for 9%

profile of v3, /device:TPU:0, one launch (start us, length us, event | category | flops | bytes accessed | tf_op | source)
XLA Modules:
  0.0 411.7 jit_solution(17717190141752714015)
XLA Ops:
  9.1 18.7 %all_gather.12 = bf16[96,3200]{1,0:T(8,128)(2,1)} all-gather(bf16[24,3200]{1,0:T(8,128)(2,1)S(1)} %concatenate.20), channel_id=1, replica_groups=mesh['dp'=2,'seq'=4,'expert'=4] {'expert'}, dimensions={0}, use_global_device_ids=true | all-gather | bytes 768000 | tf_op jit(solution)/shard_map/all_gather | solution.py:312
  32.5 2.5 convolution_convert_fusion.6
  35.0 5.2 %all-to-all-start = ((bf16[4,192,768]{2,1,0:T(8,128)(2,1)}), bf16[4,192,768]{2,1,0:T(8,128)(2,1)S(1)}, u32[]{:S(2)}, u32[]{:S(2)}) async-start(bf16[4,192,768]{2,1,0:T(8,128)(2,1)} %bitcast.6), calls=%async_computation | async-start | bytes 2359296 | tf_op jit(solution)/shard_map/all_to_all | solution.py:285
  40.6 24.9 %all-to-all-done = bf16[4,192,768]{2,1,0:T(8,128)(2,1)S(1)} async-done(((bf16[4,192,768]{2,1,0:T(8,128)(2,1)}), bf16[4,192,768]{2,1,0:T(8,128)(2,1)S(1)}, u32[]{:S(2)}, u32[]{:S(2)}) %all-to-all-start) | async-done | bytes 1179680 | tf_op jit(solution)/shard_map/all_to_all | solution.py:285
  65.5 3.7 all-gather.4.cloned.1.call-done
  69.3 3.1 convolution_convert_fusion.3.q_ref
  74.7 24.8 %collective-permute-done.1 = bf16[256,1536]{1,0:T(8,128)(2,1)} collective-permute-done((bf16[256,1536]{1,0:T(8,128)(2,1)S(1)}, bf16[256,1536]{1,0:T(8,128)(2,1)}, u32[]{:S(2)}, u32[]{:S(2)}) %collective-permute-start.1) | collective-permute-done | bytes 786464 | tf_op jit(solution)/shard_map/ppermute | solution.py:258
  99.7 3.6 collective-permute-done.2
  105.1 14.5 %shard_map.169 = bf16[256,768]{1,0:T(8,128)(2,1)S(1)} custom-call(s32[1]{0:T(128)} %bitcast.1.place_ref, f32[32,12]{1,0:T(8,128)S(1)} %copy.74.table_ref, bf16[256,2304]{1,0:T(8,128)(2,1)S(1)} %copy-done.2, bf16[1024,1536]{1,0:T(8,128)(2,1)S(1)} %pad_maximum_fusion.1.k_ref.v_ref, bf16[1024,1536]{1,0:T(8,128)(2,1)S(1)} %pad_maximum_fusion.1.k_ref.v_ref), custom_call_target="tpu_custom_call" | custom-call | flops 1610612736 | bytes 3932160 | tf_op jit(solution)/shard_map/pallas_call | solution.py:207
  124.0 4.6 %all-to-all-start.1 = ((bf16[4,192,768]{2,1,0:T(8,128)(2,1)}), bf16[4,192,768]{2,1,0:T(8,128)(2,1)S(1)}, u32[]{:S(2)}, u32[]{:S(2)}) async-start(bf16[4,192,768]{2,1,0:T(8,128)(2,1)} %bitcast.118), calls=%async_computation.1 | async-start | bytes 2359296 | tf_op jit(solution)/shard_map/all_to_all | solution.py:285
  130.2 27.3 %all-to-all-done.1 = bf16[4,192,768]{2,1,0:T(8,128)(2,1)S(1)} async-done(((bf16[4,192,768]{2,1,0:T(8,128)(2,1)}), bf16[4,192,768]{2,1,0:T(8,128)(2,1)S(1)}, u32[]{:S(2)}, u32[]{:S(2)}) %all-to-all-start.1) | async-done | bytes 1179680 | tf_op jit(solution)/shard_map/all_to_all | solution.py:285
  158.2 3.4 all-to-all-start.3
  161.7 11.0 %multiply_convert_fusion = (bf16[768,3072]{1,0:T(8,128)(2,1)}, f32[768,3072]{1,0:T(8,128)}) fusion(bf16[768,768]{1,0:T(8,128)(2,1)S(1)} %bitcast.114, bf16[1,768,3072]{2,1,0:T(8,128)(2,1)} %all-gather.6.cloned.1.call-done), kind=kOutput, calls=%fused_computation.12 | convolution fusion | flops 3645112320 | bytes 20054016 | tf_op jit(solution)/shard_map/dot_general | solution.py:361
  172.8 8.6 %fusion.28 = bf16[768,768]{1,0:T(8,128)(2,1)} fusion(bf16[768,3072]{1,0:T(8,128)(2,1)} %get-tuple-element.28, bf16[1,3072,768]{1,2,0:T(8,128)(2,1)} %all-gather.8.cloned.1.call-done), kind=kOutput, calls=%fused_computation.37 | convolution fusion | flops 3624468480 | bytes 10616832 | tf_op jit(solution)/shard_map/dot_general | solution.py:363
  181.4 4.8 %all-to-all-start.2 = ((bf16[4,192,768]{2,1,0:T(8,128)(2,1)}), bf16[4,192,768]{2,1,0:T(8,128)(2,1)S(1)}, u32[]{:S(2)}, u32[]{:S(2)}) async-start(bf16[4,192,768]{2,1,0:T(8,128)(2,1)} %bitcast.117), calls=%async_computation.2 | async-start | bytes 2359296 | tf_op jit(solution)/shard_map/all_to_all | solution.py:285
  186.3 13.0 %fusion.7 = bf16[768,3072]{1,0:T(8,128)(2,1)S(1)} fusion(f32[768,3072]{1,0:T(8,128)} %get-tuple-element.115, bf16[1,3072,768]{1,2,0:T(8,128)(2,1)} %all-gather.8.cloned.1.call-done, bf16[768,768]{1,0:T(8,128)(2,1)S(1)} %bitcast.112, f32[768]{0:T(1024)S(1)} %mul.234), kind=kOutput, calls=%fused_computation.10 | convolution fusion | flops 3672834048 | bytes 20057088 | tf_op jit(solution)/shard_map/rd,fd->rf/dot_general | solution.py:368
  199.3 7.3 %fusion.25 = bf16[768,768]{1,0:T(8,128)(2,1)} fusion(bf16[768,3072]{1,0:T(8,128)(2,1)S(1)} %fusion.7, bf16[1,768,3072]{2,1,0:T(8,128)(2,1)} %all-gather.6.cloned.1.call-done), kind=kOutput, calls=%fused_computation.36 | convolution fusion | flops 3624468480 | bytes 10616832 | tf_op jit(solution)/shard_map/rf,df->rd/dot_general | solution.py:373
  206.6 4.1 %convolution_convert_fusion.2 = bf16[768,3072]{1,0:T(8,128)(2,1)S(1)} fusion(bf16[768,768]{1,0:T(8,128)(2,1)S(1)} %bitcast.115, bf16[768,3072]{1,0:T(8,128)(2,1)S(1)} %fusion.7), kind=kOutput, calls=%fused_computation.15 | convolution fusion | flops 3626237952 | bytes 10616832 | tf_op jit(solution)/shard_map/dot_general | solution.py:378
  210.8 6.6 %convolution_convert_fusion.1 = bf16[768,3072]{1,0:T(8,128)(2,1)S(1)} fusion(bf16[768,3072]{1,0:T(8,128)(2,1)} %get-tuple-element.28, bf16[768,768]{1,0:T(8,128)(2,1)S(1)} %bitcast.113, f32[768]{0:T(1024)S(1)} %mul.234), kind=kOutput, calls=%fused_computation.14 | convolution fusion | flops 3628007424 | bytes 10619904 | tf_op jit(solution)/shard_map/dot_general | solution.py:381
  217.4 3.9 pad_maximum_fusion
  221.4 5.2 %all-to-all-start.4 = ((bf16[4,192,768]{2,1,0:T(8,128)(2,1)}), bf16[4,192,768]{2,1,0:T(8,128)(2,1)}, u32[]{:S(2)}, u32[]{:S(2)}) async-start(bf16[4,192,768]{2,1,0:T(8,128)(2,1)} %bitcast.116), calls=%async_computation.4 | async-start | bytes 2359296 | tf_op jit(solution)/shard_map/all_to_all | solution.py:285
  228.6 25.0 %all-to-all-done.4 = bf16[4,192,768]{2,1,0:T(8,128)(2,1)} async-done(((bf16[4,192,768]{2,1,0:T(8,128)(2,1)}), bf16[4,192,768]{2,1,0:T(8,128)(2,1)}, u32[]{:S(2)}, u32[]{:S(2)}) %all-to-all-start.4) | async-done | bytes 1179680 | tf_op jit(solution)/shard_map/all_to_all | solution.py:285
  255.6 2.2 multiply_reduce_fusion
  260.8 24.1 %shard_map.170 = (bf16[256,768]{1,0:T(8,128)(2,1)S(1)}, bf16[4,2,256,768]{3,2,1,0:T(8,128)(2,1)S(1)}, f32[12,32,128]{2,1,0:T(8,128)S(1)}) custom-call(s32[1]{0:T(128)} %bitcast.1.place_ref, f32[32,12]{1,0:T(8,128)S(1)} %copy.74.table_ref, bf16[256,2304]{1,0:T(8,128)(2,1)S(1)} %copy-done.3, bf16[1024,1536]{1,0:T(8,128)(2,1)} %copy-done, ...), custom_call_target="tpu_custom_call" | custom-call | flops 4026531840 | bytes 7471104 | tf_op jit(solution)/shard_map/pallas_call | solution.py:227
  287.9 2.9 collective-permute-done.4
  294.2 2.7 convolution_convert_fusion.4
  296.9 16.9 %collective-permute-done.5 = bf16[2,256,768]{2,1,0:T(8,128)(2,1)} collective-permute-done((bf16[2,256,768]{2,1,0:T(8,128)(2,1)}, bf16[2,256,768]{2,1,0:T(8,128)(2,1)}, u32[]{:S(2)}, u32[]{:S(2)}) %collective-permute-start.5) | collective-permute-done | bytes 786464 | tf_op jit(solution)/shard_map/ppermute | solution.py:258
  317.9 2.6 fusion.8
  321.7 4.7 %fusion.45 = (f32[768]{0:T(1024)S(1)}, f32[256]{0:T(256)}, f32[256,768]{1,0:T(8,128)}) fusion(bf16[1,256,768]{2,1,0:T(8,128)(2,1)S(1)} %copy-done.16, f32[256]{0:T(256)} %copy-done.28, f32[768]{0:T(1024)S(1)} %copy-done.24, bf16[256,2304]{1,0:T(8,128)(2,1)S(1)} %pad_maximum_fusion.2, bf16[768,3200]{1,0:T(8,128)(2,1)} %all-gather.4.cloned.1.call-done), kind=kOutput, calls=%fused_computation.66 | convolution fusion | flops 907344896 | bytes 5906432 | tf_op jit(solution)/shard_map/qe,de->qd/dot_general | solution.py:435
  326.4 39.6 %all-reduce.2 = (f32[2,768]{1,0:T(2,128)}, f32[32,12]{0,1:T(8,128)}) all-reduce(f32[2,768]{1,0:T(2,128)S(1)} %pad_maximum_fusion.3, f32[32,12]{0,1:T(8,128)S(1)} %bitcast.119), channel_id=1, replica_groups=mesh['dp'=2,'seq'=4,'expert'=4] {'dp','seq','expert'}, use_global_device_ids=true, to_apply=%region_20.21 | all-reduce | flops 1920 | bytes 15360 | tf_op jit(solution)/shard_map/psum | solution.py:440
  366.0 9.7 %reduce-scatter.8.cloned.1.call-done = bf16[96,3200]{1,0:T(8,128)(2,1)} async-done(((bf16[768,3200]{1,0:T(8,128)(2,1)}), bf16[96,3200]{1,0:T(8,128)(2,1)}) %reduce-scatter.8.cloned.1.call-update) | async-done | bytes 614416 | tf_op jit(solution)/shard_map/reduce_scatter | solution.py:427
  380.2 20.3 %reduce-scatter.10.cloned.1.call-done = bf16[24,3200]{1,0:T(8,128)(2,1)} async-done(((bf16[96,3200]{1,0:T(8,128)(2,1)}), bf16[24,3200]{1,0:T(8,128)(2,1)}) %reduce-scatter.10.cloned.1.call-update) | async-done | bytes 153616
  (152 shorter events, 45.1 us)
Async XLA Ops:
  7.2 33.0 %copy-start.30 = (f32[2,768]{1,0:T(2,128)S(1)}, f32[2,768]{1,0:T(2,128)}, u32[]{:S(2)}) copy-start(f32[2,768]{1,0:T(2,128)} %param.16) | copy-start | bytes 18436
  7.2 33.0 %copy-start.15 = (bf16[1,256,768]{2,1,0:T(8,128)(2,1)S(1)}, bf16[1,256,768]{2,1,0:T(8,128)(2,1)}, u32[]{:S(2)}) copy-start(bf16[1,256,768]{2,1,0:T(8,128)(2,1)} %param.10) | copy-start | bytes 1179652
  7.2 62.1 %all-gather.4.cloned.1.call-start = ((), (), s32[]{:S(2)}) async-start(), calls=%async_computation.8 | async-start | bytes 5529600 | tf_op jit(solution)/shard_map/all_gather | solution.py:313
  27.8 133.9 %all-gather.6.cloned.1.call-start = ((), (), s32[]{:S(2)}) async-start(), calls=%async_computation.9 | async-start | bytes 5308416 | tf_op jit(solution)/shard_map/all_gather | solution.py:339
  28.5 144.2 %all-gather.8.cloned.1.call-start = ((), (), s32[]{:S(2)}) async-start(), calls=%async_computation.10 | async-start | bytes 5308416 | tf_op jit(solution)/shard_map/all_gather | solution.py:340
  35.0 30.6 %all-to-all-start = ((bf16[4,192,768]{2,1,0:T(8,128)(2,1)}), bf16[4,192,768]{2,1,0:T(8,128)(2,1)S(1)}, u32[]{:S(2)}, u32[]{:S(2)}) async-start(bf16[4,192,768]{2,1,0:T(8,128)(2,1)} %bitcast.6), calls=%async_computation | async-start | bytes 2359296 | tf_op jit(solution)/shard_map/all_to_all | solution.py:285
  40.2 32.2 %copy-start.23 = (f32[768]{0:T(1024)}, f32[768]{0:T(1024)S(1)}, u32[]{:S(2)}) copy-start(f32[768]{0:T(1024)S(1)} %get-tuple-element.100) | copy-start | bytes 9220
  40.3 59.3 %copy-start.29 = (f32[32,12]{0,1:T(8,128)S(1)}, f32[32,12]{0,1:T(8,128)}, u32[]{:S(2)}) copy-start(f32[32,12]{0,1:T(8,128)} %param.17) | copy-start | bytes 4612
  40.4 59.1 %copy-start.28 = (f32[256]{0:T(256)}, f32[256]{0:T(256)S(1)}, u32[]{:S(2)}) copy-start(f32[256]{0:T(256)S(1)} %add_rsqrt_fusion.1) | copy-start | bytes 3076
  40.6 64.5 %copy-start.17 = (bf16[256,768]{1,0:T(8,128)(2,1)}, bf16[256,768]{1,0:T(8,128)(2,1)S(1)}, u32[]{:S(2)}) copy-start(bf16[256,768]{1,0:T(8,128)(2,1)S(1)} %fusion.39) | copy-start | bytes 1179652
  73.4 26.1 %collective-permute-start.1 = (bf16[256,1536]{1,0:T(8,128)(2,1)S(1)}, bf16[256,1536]{1,0:T(8,128)(2,1)}, u32[]{:S(2)}, u32[]{:S(2)}) collective-permute-start(bf16[256,1536]{1,0:T(8,128)(2,1)S(1)} %slice.100), channel_id=1, source_target_pairs={{0,8},{4,12},{8,0},{12,4},{1,9},{5,13},{9,1},{13,5},{2,10},{6,14},... | collective-permute-start | bytes 2359304 | tf_op jit(solution)/shard_map/ppermute | solution.py:258
  74.7 24.9 %collective-permute-start = (bf16[256,1536]{1,0:T(8,128)(2,1)S(1)}, bf16[256,1536]{1,0:T(8,128)(2,1)}, u32[]{:S(2)}, u32[]{:S(2)}) collective-permute-start(bf16[256,1536]{1,0:T(8,128)(2,1)S(1)} %slice.100), channel_id=1, source_target_pairs={{0,4},{4,0},{8,12},{12,8},{1,5},{5,1},{9,13},{13,9},{2,6},{6,2},{1... | collective-permute-start | bytes 2359304 | tf_op jit(solution)/shard_map/ppermute | solution.py:258
  99.6 3.8 collective-permute-start.2
  105.1 16.3 %copy-start = (bf16[1024,1536]{1,0:T(8,128)(2,1)}, bf16[1024,1536]{1,0:T(8,128)(2,1)S(1)}, u32[]{:S(2)}) copy-start(bf16[1024,1536]{1,0:T(8,128)(2,1)S(1)} %pad_maximum_fusion.1.k_ref.v_ref) | copy-start | bytes 9437188
  122.5 50.3 %copy-start.13 = (bf16[256,768]{1,0:T(8,128)(2,1)}, bf16[256,768]{1,0:T(8,128)(2,1)S(1)}, u32[]{:S(2)}) copy-start(bf16[256,768]{1,0:T(8,128)(2,1)S(1)} %multiply_convert_fusion.2) | copy-start | bytes 1179652
  124.0 33.5 %all-to-all-start.1 = ((bf16[4,192,768]{2,1,0:T(8,128)(2,1)}), bf16[4,192,768]{2,1,0:T(8,128)(2,1)S(1)}, u32[]{:S(2)}, u32[]{:S(2)}) async-start(bf16[4,192,768]{2,1,0:T(8,128)(2,1)} %bitcast.118), calls=%async_computation.1 | async-start | bytes 2359296 | tf_op jit(solution)/shard_map/all_to_all | solution.py:285
  157.5 15.3 %copy-start.20 = (bf16[4,192,768]{2,1,0:T(8,128)(2,1)}, bf16[4,192,768]{2,1,0:T(8,128)(2,1)S(1)}, u32[]{:S(2)}) copy-start(bf16[4,192,768]{2,1,0:T(8,128)(2,1)S(1)} %all-to-all-done.1) | copy-start | bytes 3538948
  158.2 23.2 %all-to-all-start.3 = ((f32[4,1,192]{2,1,0:T(1,128)}), f32[4,1,192]{2,1,0:T(1,128)S(1)}, u32[]{:S(2)}, u32[]{:S(2)}) async-start(f32[4,1,192]{2,1,0:T(1,128)} %all_to_all.21), calls=%async_computation.3 | async-start | bytes 8192 | tf_op jit(solution)/shard_map/all_to_all | solution.py:354
  181.4 39.9 %all-to-all-start.2 = ((bf16[4,192,768]{2,1,0:T(8,128)(2,1)}), bf16[4,192,768]{2,1,0:T(8,128)(2,1)S(1)}, u32[]{:S(2)}, u32[]{:S(2)}) async-start(bf16[4,192,768]{2,1,0:T(8,128)(2,1)} %bitcast.117), calls=%async_computation.2 | async-start | bytes 2359296 | tf_op jit(solution)/shard_map/all_to_all | solution.py:285
  186.2 129.5 %reduce-scatter.6.cloned.1.call-start = ((), (), s32[]{:S(2)}) async-start(), calls=%async_computation.11 | async-start | bytes 10616832 | tf_op jit(solution)/shard_map/reduce_scatter | solution.py:415
  199.3 7.3 %copy-start.21 = (bf16[4,192,768]{2,1,0:T(8,128)(2,1)S(1)}, bf16[4,192,768]{2,1,0:T(8,128)(2,1)}, u32[]{:S(2)}) copy-start(bf16[4,192,768]{2,1,0:T(8,128)(2,1)} %copy-done.20) | copy-start | bytes 3538948
  221.4 32.3 %all-to-all-start.4 = ((bf16[4,192,768]{2,1,0:T(8,128)(2,1)}), bf16[4,192,768]{2,1,0:T(8,128)(2,1)}, u32[]{:S(2)}, u32[]{:S(2)}) async-start(bf16[4,192,768]{2,1,0:T(8,128)(2,1)} %bitcast.116), calls=%async_computation.4 | async-start | bytes 2359296 | tf_op jit(solution)/shard_map/all_to_all | solution.py:285
  226.6 149.1 %reduce-scatter.8.cloned.1.call-start = ((), (), s32[]{:S(2)}) async-start(), calls=%async_computation.12 | async-start | bytes 5529600 | tf_op jit(solution)/shard_map/reduce_scatter | solution.py:427
  228.6 29.5 %copy-start.25 = (f32[256,4]{0,1:T(4,128)}, f32[256,4]{0,1:T(4,128)S(1)}, u32[]{:S(2)}) copy-start(f32[256,4]{0,1:T(4,128)S(1)} %select_reduce_fusion) | copy-start | bytes 12292
  253.7 7.1 %copy-start.3 = (bf16[256,2304]{1,0:T(8,128)(2,1)S(1)}, bf16[256,2304]{1,0:T(8,128)(2,1)}, u32[]{:S(2)}) copy-start(bf16[256,2304]{1,0:T(8,128)(2,1)} %copy-done.1) | copy-start | bytes 3538948
  287.4 3.4 collective-permute-start.4
  287.4 9.5 %collective-permute-start.3 = (bf16[2,256,768]{2,1,0:T(8,128)(2,1)}, bf16[2,256,768]{2,1,0:T(8,128)(2,1)}, u32[]{:S(2)}, u32[]{:S(2)}) collective-permute-start(bf16[2,256,768]{2,1,0:T(8,128)(2,1)} %get-tuple-element.103), channel_id=1, source_target_pairs={{0,4},{4,0},{8,12},{12,8},{1,5},{5,1},{9,13},{13,9},{2,6},{6,2},{1... | collective-permute-start | bytes 2359304 | tf_op jit(solution)/shard_map/ppermute | solution.py:258
  291.9 22.0 %collective-permute-start.5 = (bf16[2,256,768]{2,1,0:T(8,128)(2,1)}, bf16[2,256,768]{2,1,0:T(8,128)(2,1)}, u32[]{:S(2)}, u32[]{:S(2)}) collective-permute-start(bf16[2,256,768]{2,1,0:T(8,128)(2,1)} %fusion.22), channel_id=1, source_target_pairs={{0,8},{4,12},{8,0},{12,4},{1,9},{5,13},{9,1},{13,5},{2,10},{6,14},... | collective-permute-start | bytes 2359304 | tf_op jit(solution)/shard_map/ppermute | solution.py:258
  294.2 21.4 %copy-start.5 = (bf16[256,768]{1,0:T(8,128)(2,1)S(1)}, bf16[256,768]{1,0:T(8,128)(2,1)}, u32[]{:S(2)}) copy-start(bf16[256,768]{1,0:T(8,128)(2,1)} %copy-done.4) | copy-start | bytes 1179652
  320.6 79.9 %reduce-scatter.10.cloned.1.call-start = ((), (), s32[]{:S(2)}) async-start(), calls=%async_computation.13 | async-start | bytes 768000
  321.7 54.8 %copy-start.11 = (f32[256,768]{1,0:T(8,128)S(1)}, f32[256,768]{1,0:T(8,128)}, u32[]{:S(2)}) copy-start(f32[256,768]{1,0:T(8,128)} %copy-done.10) | copy-start | bytes 2359300
  321.7 56.9 %copy-start.19 = (bf16[96,6144]{1,0:T(8,128)(2,1)S(1)}, bf16[96,6144]{1,0:T(8,128)(2,1)}, u32[]{:S(2)}) copy-start(bf16[96,6144]{1,0:T(8,128)(2,1)} %reduce-scatter.6.cloned.1.call-done) | copy-start | bytes 3538948
  (16 other events, 43.1 us)
Sparse Core Ops, SparseCore 0:
  27.9 41.3 all-gather.3
  71.1 45.4 all-gather.5
  118.6 38.9 all-gather.7
  221.5 78.9 reduce-scatter.5
  320.7 54.9 reduce-scatter.7
  378.0 22.4 reduce-scatter.9

commit v4 on v3

--- a/solution.py
+++ b/solution.py
@@ -427,9 +427,10 @@
     weight_grads = lax.psum_scatter(
         weight_parts.astype(jnp.bfloat16), ("dp", "seq"), scatter_dimension=0, tiled=True
     )
-    weight_grads = lax.psum_scatter(
-        weight_grads, "expert", scatter_dimension=0, tiled=True
-    ).astype(jnp.float32)
+    weight_grads = swap_experts(weight_grads, experts_total)
+    weight_grads = jnp.sum(
+        weight_grads.reshape(experts_total, -1, weight_grads.shape[1]).astype(jnp.float32), axis=0
+    )
     qkv_grad, out_grad = weight_grads[:, : 3 * D], weight_grads[:, 3 * D : 4 * D]
     router_grad = weight_grads[:, 4 * D : 4 * D + experts_total]
     normed_grad = jnp.einsum(

time: 413 us -> 405 us (0.981)
  waiting for transfers between devices: 161 us -> 152 us
  starting transfers between devices: 26.4 us -> 31 us
    unnamed x7 -> x5, waiting for transfers between devices: 21.7 us -> 1.43 us
    all_to_all x4 -> x5, waiting for transfers between devices: 77.2 us -> 89.8 us  [swap_experts(): lax.all_to_all(slots.reshape(experts_total, slots.shape[0] // experts_tot...]
    all_to_all x4 -> x5, starting transfers between devices: 19.9 us -> 24.4 us  [swap_experts(): lax.all_to_all(slots.reshape(experts_total, slots.shape[0] // experts_tot...]
    unnamed x67 -> x69, local copies, waits for them, and re-layouts: 8.43 us -> 8.48 us
  transfers between devices with their start and end apart: 17 -> 17, of which waited for: 10 -> 10; matrix products, arithmetic and copies ran while one was open for 23% -> 24% of each run, Pallas kernels for 9% -> 10%
where the time goes in v4:
time: 405 us; the launch traced here: 404 us
  waiting for transfers between devices  152 us (38%)
  matrix products  77.5 us (19%)
  blocking collectives  58.3 us (14%)
  Pallas kernels  38.6 us (10%)
  starting transfers between devices  31 us (8%)
  other arithmetic  18.4 us (5%)
  between operations  14.3 us (4%)
  local copies, waits for them, and re-layouts  13.7 us (3%)
    all_to_all x5, waiting for transfers between devices, swap_experts(): lax.all_to_all(slots.reshape(experts_total, slots.shape[0] // experts_tot...  89.8 us
    ppermute x6, waiting for transfers between devices, swap_pairs(): return lax.ppermute(block, 'seq', pairs)  48.3 us
    psum x1, blocking collectives, local(): lax.psum((jnp.stack([gain_one, gain_two]), jnp.sum(bucket_rows, axis=-1)....  39.6 us
    all_to_all x5, starting transfers between devices, swap_experts(): lax.all_to_all(slots.reshape(experts_total, slots.shape[0] // experts_tot...  24.4 us
    pallas_call x1, Pallas kernels, attend_back(): pl.pallas_call(functools.partial(attend_back_kernel, tiles), grid=(pairs,...  24.1 us
    all_gather x1, blocking collectives, local(): packed = lax.all_gather(packed, 'expert', axis=0, tiled=True)  18.7 us
    pallas_call x1, Pallas kernels, attend(): pl.pallas_call(functools.partial(attend_kernel, tiles), grid=(pairs,), ou...  14.5 us
    dot_general x1, matrix products, local(): jnp.einsum('rd,fd->rf', arrived_grad, w_out_full, preferred_element_type=...  13 us
  transfers between devices with their start and end apart: 17, of which 10 were waited for; matrix products, arithmetic and copies ran while one was open for 24% of the time, Pallas kernels for 10%

profile of v4, /device:TPU:0, one launch (start us, length us, event | category | flops | bytes accessed | tf_op | source)
XLA Modules:
  0.0 404.3 jit_solution(13737081527518522993)
XLA Ops:
  9.1 18.7 %all_gather.12 = bf16[96,3200]{1,0:T(8,128)(2,1)} all-gather(bf16[24,3200]{1,0:T(8,128)(2,1)S(1)} %concatenate.20), channel_id=1, replica_groups=mesh['dp'=2,'seq'=4,'expert'=4] {'expert'}, dimensions={0}, use_global_device_ids=true | all-gather | bytes 768000 | tf_op jit(solution)/shard_map/all_gather | solution.py:312
  32.5 2.5 convolution_convert_fusion.6
  35.0 5.2 %all-to-all-start = ((bf16[4,192,768]{2,1,0:T(8,128)(2,1)}), bf16[4,192,768]{2,1,0:T(8,128)(2,1)S(1)}, u32[]{:S(2)}, u32[]{:S(2)}) async-start(bf16[4,192,768]{2,1,0:T(8,128)(2,1)} %bitcast.6), calls=%async_computation | async-start | bytes 2359296 | tf_op jit(solution)/shard_map/all_to_all | solution.py:285
  40.6 24.9 %all-to-all-done = bf16[4,192,768]{2,1,0:T(8,128)(2,1)S(1)} async-done(((bf16[4,192,768]{2,1,0:T(8,128)(2,1)}), bf16[4,192,768]{2,1,0:T(8,128)(2,1)S(1)}, u32[]{:S(2)}, u32[]{:S(2)}) %all-to-all-start) | async-done | bytes 1179680 | tf_op jit(solution)/shard_map/all_to_all | solution.py:285
  65.5 3.7 all-gather.4.cloned.1.call-done
  69.3 3.1 convolution_convert_fusion.3.q_ref
  74.7 24.8 %collective-permute-done.1 = bf16[256,1536]{1,0:T(8,128)(2,1)} collective-permute-done((bf16[256,1536]{1,0:T(8,128)(2,1)S(1)}, bf16[256,1536]{1,0:T(8,128)(2,1)}, u32[]{:S(2)}, u32[]{:S(2)}) %collective-permute-start.1) | collective-permute-done | bytes 786464 | tf_op jit(solution)/shard_map/ppermute | solution.py:258
  99.7 3.6 collective-permute-done.2
  105.1 14.5 %shard_map.169 = bf16[256,768]{1,0:T(8,128)(2,1)S(1)} custom-call(s32[1]{0:T(128)} %bitcast.1.place_ref, f32[32,12]{1,0:T(8,128)S(1)} %copy.77.table_ref, bf16[256,2304]{1,0:T(8,128)(2,1)S(1)} %copy-done.2, bf16[1024,1536]{1,0:T(8,128)(2,1)S(1)} %pad_maximum_fusion.1.k_ref.v_ref, bf16[1024,1536]{1,0:T(8,128)(2,1)S(1)} %pad_maximum_fusion.1.k_ref.v_ref), custom_call_target="tpu_custom_call" | custom-call | flops 1610612736 | bytes 3932160 | tf_op jit(solution)/shard_map/pallas_call | solution.py:207
  124.0 4.6 %all-to-all-start.1 = ((bf16[4,192,768]{2,1,0:T(8,128)(2,1)}), bf16[4,192,768]{2,1,0:T(8,128)(2,1)S(1)}, u32[]{:S(2)}, u32[]{:S(2)}) async-start(bf16[4,192,768]{2,1,0:T(8,128)(2,1)} %bitcast.118), calls=%async_computation.1 | async-start | bytes 2359296 | tf_op jit(solution)/shard_map/all_to_all | solution.py:285
  130.2 27.3 %all-to-all-done.1 = bf16[4,192,768]{2,1,0:T(8,128)(2,1)S(1)} async-done(((bf16[4,192,768]{2,1,0:T(8,128)(2,1)}), bf16[4,192,768]{2,1,0:T(8,128)(2,1)S(1)}, u32[]{:S(2)}, u32[]{:S(2)}) %all-to-all-start.1) | async-done | bytes 1179680 | tf_op jit(solution)/shard_map/all_to_all | solution.py:285
  158.2 3.4 all-to-all-start.3
  161.7 11.0 %multiply_convert_fusion = (bf16[768,3072]{1,0:T(8,128)(2,1)}, f32[768,3072]{1,0:T(8,128)}) fusion(bf16[768,768]{1,0:T(8,128)(2,1)S(1)} %bitcast.114, bf16[1,768,3072]{2,1,0:T(8,128)(2,1)} %all-gather.6.cloned.1.call-done), kind=kOutput, calls=%fused_computation.12 | convolution fusion | flops 3645112320 | bytes 20054016 | tf_op jit(solution)/shard_map/dot_general | solution.py:361
  172.8 8.6 %fusion.28 = bf16[768,768]{1,0:T(8,128)(2,1)} fusion(bf16[768,3072]{1,0:T(8,128)(2,1)} %get-tuple-element.28, bf16[1,3072,768]{1,2,0:T(8,128)(2,1)} %all-gather.8.cloned.1.call-done), kind=kOutput, calls=%fused_computation.37 | convolution fusion | flops 3624468480 | bytes 10616832 | tf_op jit(solution)/shard_map/dot_general | solution.py:363
  181.4 4.8 %all-to-all-start.2 = ((bf16[4,192,768]{2,1,0:T(8,128)(2,1)}), bf16[4,192,768]{2,1,0:T(8,128)(2,1)S(1)}, u32[]{:S(2)}, u32[]{:S(2)}) async-start(bf16[4,192,768]{2,1,0:T(8,128)(2,1)} %bitcast.117), calls=%async_computation.2 | async-start | bytes 2359296 | tf_op jit(solution)/shard_map/all_to_all | solution.py:285
  186.3 13.0 %fusion.7 = bf16[768,3072]{1,0:T(8,128)(2,1)S(1)} fusion(f32[768,3072]{1,0:T(8,128)} %get-tuple-element.115, bf16[1,3072,768]{1,2,0:T(8,128)(2,1)} %all-gather.8.cloned.1.call-done, bf16[768,768]{1,0:T(8,128)(2,1)S(1)} %bitcast.112, f32[768]{0:T(1024)S(1)} %mul.234), kind=kOutput, calls=%fused_computation.10 | convolution fusion | flops 3672834048 | bytes 20057088 | tf_op jit(solution)/shard_map/rd,fd->rf/dot_general | solution.py:368
  199.3 7.3 %fusion.25 = bf16[768,768]{1,0:T(8,128)(2,1)} fusion(bf16[768,3072]{1,0:T(8,128)(2,1)S(1)} %fusion.7, bf16[1,768,3072]{2,1,0:T(8,128)(2,1)} %all-gather.6.cloned.1.call-done), kind=kOutput, calls=%fused_computation.36 | convolution fusion | flops 3624468480 | bytes 10616832 | tf_op jit(solution)/shard_map/rf,df->rd/dot_general | solution.py:373
  206.6 4.1 %convolution_convert_fusion.2 = bf16[768,3072]{1,0:T(8,128)(2,1)S(1)} fusion(bf16[768,768]{1,0:T(8,128)(2,1)S(1)} %bitcast.115, bf16[768,3072]{1,0:T(8,128)(2,1)S(1)} %fusion.7), kind=kOutput, calls=%fused_computation.15 | convolution fusion | flops 3626237952 | bytes 10616832 | tf_op jit(solution)/shard_map/dot_general | solution.py:378
  210.8 6.6 %convolution_convert_fusion.1 = bf16[768,3072]{1,0:T(8,128)(2,1)S(1)} fusion(bf16[768,3072]{1,0:T(8,128)(2,1)} %get-tuple-element.28, bf16[768,768]{1,0:T(8,128)(2,1)S(1)} %bitcast.113, f32[768]{0:T(1024)S(1)} %mul.234), kind=kOutput, calls=%fused_computation.14 | convolution fusion | flops 3628007424 | bytes 10619904 | tf_op jit(solution)/shard_map/dot_general | solution.py:381
  217.4 3.9 pad_maximum_fusion
  221.4 5.2 %all-to-all-start.4 = ((bf16[4,192,768]{2,1,0:T(8,128)(2,1)}), bf16[4,192,768]{2,1,0:T(8,128)(2,1)}, u32[]{:S(2)}, u32[]{:S(2)}) async-start(bf16[4,192,768]{2,1,0:T(8,128)(2,1)} %bitcast.116), calls=%async_computation.4 | async-start | bytes 2359296 | tf_op jit(solution)/shard_map/all_to_all | solution.py:285
  228.6 25.0 %all-to-all-done.4 = bf16[4,192,768]{2,1,0:T(8,128)(2,1)} async-done(((bf16[4,192,768]{2,1,0:T(8,128)(2,1)}), bf16[4,192,768]{2,1,0:T(8,128)(2,1)}, u32[]{:S(2)}, u32[]{:S(2)}) %all-to-all-start.4) | async-done | bytes 1179680 | tf_op jit(solution)/shard_map/all_to_all | solution.py:285
  260.8 24.1 %shard_map.170 = (bf16[256,768]{1,0:T(8,128)(2,1)S(1)}, bf16[4,2,256,768]{3,2,1,0:T(8,128)(2,1)S(1)}, f32[12,32,128]{2,1,0:T(8,128)S(1)}) custom-call(s32[1]{0:T(128)} %bitcast.1.place_ref, f32[32,12]{1,0:T(8,128)S(1)} %copy.77.table_ref, bf16[256,2304]{1,0:T(8,128)(2,1)S(1)} %copy-done.3, bf16[1024,1536]{1,0:T(8,128)(2,1)} %copy-done, ...), custom_call_target="tpu_custom_call" | custom-call | flops 4026531840 | bytes 7471104 | tf_op jit(solution)/shard_map/pallas_call | solution.py:227
  287.9 2.9 collective-permute-done.4
  294.2 2.7 convolution_convert_fusion.4
  296.9 16.9 %collective-permute-done.5 = bf16[2,256,768]{2,1,0:T(8,128)(2,1)} collective-permute-done((bf16[2,256,768]{2,1,0:T(8,128)(2,1)}, bf16[2,256,768]{2,1,0:T(8,128)(2,1)}, u32[]{:S(2)}, u32[]{:S(2)}) %collective-permute-start.5) | collective-permute-done | bytes 786464 | tf_op jit(solution)/shard_map/ppermute | solution.py:258
  316.9 2.6 fusion.8
  320.6 4.7 %fusion.45 = (f32[768]{0:T(1024)S(1)}, f32[256]{0:T(256)}, f32[256,768]{1,0:T(8,128)}) fusion(bf16[1,256,768]{2,1,0:T(8,128)(2,1)S(1)} %copy-done.16, f32[256]{0:T(256)} %copy-done.29, f32[768]{0:T(1024)S(1)} %copy-done.25, bf16[256,2304]{1,0:T(8,128)(2,1)S(1)} %pad_maximum_fusion.2, bf16[768,3200]{1,0:T(8,128)(2,1)} %all-gather.4.cloned.1.call-done), kind=kOutput, calls=%fused_computation.67 | convolution fusion | flops 907344896 | bytes 5906432 | tf_op jit(solution)/shard_map/qe,de->qd/dot_general | solution.py:436
  325.3 39.6 %all-reduce.1 = (f32[2,768]{1,0:T(2,128)}, f32[32,12]{0,1:T(8,128)}) all-reduce(f32[2,768]{1,0:T(2,128)S(1)} %pad_maximum_fusion.3, f32[32,12]{0,1:T(8,128)S(1)} %bitcast.120), channel_id=1, replica_groups=mesh['dp'=2,'seq'=4,'expert'=4] {'dp','seq','expert'}, use_global_device_ids=true, to_apply=%region_20.21 | all-reduce | flops 1920 | bytes 15360 | tf_op jit(solution)/shard_map/psum | solution.py:441
  365.6 9.0 %reduce-scatter.5.cloned.1.call-done = bf16[96,3200]{1,0:T(8,128)(2,1)} async-done(((bf16[768,3200]{1,0:T(8,128)(2,1)}), bf16[96,3200]{1,0:T(8,128)(2,1)}) %reduce-scatter.5.cloned.1.call-update) | async-done | bytes 614416 | tf_op jit(solution)/shard_map/reduce_scatter | solution.py:427
  374.6 4.6 %all-to-all-start.5 = ((bf16[4,24,3200]{2,1,0:T(8,128)(2,1)}), bf16[4,24,3200]{2,1,0:T(8,128)(2,1)S(1)}, u32[]{:S(2)}, u32[]{:S(2)}) async-start(bf16[4,24,3200]{2,1,0:T(8,128)(2,1)} %bitcast.119), calls=%async_computation.7 | async-start | bytes 1228800 | tf_op jit(solution)/shard_map/all_to_all | solution.py:285
  383.0 12.6 %all-to-all-done.5 = bf16[4,24,3200]{2,1,0:T(8,128)(2,1)S(1)} async-done(((bf16[4,24,3200]{2,1,0:T(8,128)(2,1)}), bf16[4,24,3200]{2,1,0:T(8,128)(2,1)S(1)}, u32[]{:S(2)}, u32[]{:S(2)}) %all-to-all-start.5) | async-done | bytes 614432 | tf_op jit(solution)/shard_map/all_to_all | solution.py:285
  (154 shorter events, 44.0 us)
Async XLA Ops:
  7.2 33.0 %copy-start.31 = (f32[2,768]{1,0:T(2,128)S(1)}, f32[2,768]{1,0:T(2,128)}, u32[]{:S(2)}) copy-start(f32[2,768]{1,0:T(2,128)} %param.16) | copy-start | bytes 18436
  7.2 33.0 %copy-start.15 = (bf16[1,256,768]{2,1,0:T(8,128)(2,1)S(1)}, bf16[1,256,768]{2,1,0:T(8,128)(2,1)}, u32[]{:S(2)}) copy-start(bf16[1,256,768]{2,1,0:T(8,128)(2,1)} %param.10) | copy-start | bytes 1179652
  7.2 62.1 %all-gather.4.cloned.1.call-start = ((), (), s32[]{:S(2)}) async-start(), calls=%async_computation.8 | async-start | bytes 5529600 | tf_op jit(solution)/shard_map/all_gather | solution.py:313
  27.8 133.9 %all-gather.6.cloned.1.call-start = ((), (), s32[]{:S(2)}) async-start(), calls=%async_computation.9 | async-start | bytes 5308416 | tf_op jit(solution)/shard_map/all_gather | solution.py:339
  28.5 144.2 %all-gather.8.cloned.1.call-start = ((), (), s32[]{:S(2)}) async-start(), calls=%async_computation.10 | async-start | bytes 5308416 | tf_op jit(solution)/shard_map/all_gather | solution.py:340
  35.0 30.6 %all-to-all-start = ((bf16[4,192,768]{2,1,0:T(8,128)(2,1)}), bf16[4,192,768]{2,1,0:T(8,128)(2,1)S(1)}, u32[]{:S(2)}, u32[]{:S(2)}) async-start(bf16[4,192,768]{2,1,0:T(8,128)(2,1)} %bitcast.6), calls=%async_computation | async-start | bytes 2359296 | tf_op jit(solution)/shard_map/all_to_all | solution.py:285
  40.2 32.2 %copy-start.24 = (f32[768]{0:T(1024)}, f32[768]{0:T(1024)S(1)}, u32[]{:S(2)}) copy-start(f32[768]{0:T(1024)S(1)} %get-tuple-element.100) | copy-start | bytes 9220
  40.3 59.3 %copy-start.30 = (f32[32,12]{0,1:T(8,128)S(1)}, f32[32,12]{0,1:T(8,128)}, u32[]{:S(2)}) copy-start(f32[32,12]{0,1:T(8,128)} %param.17) | copy-start | bytes 4612
  40.4 59.1 %copy-start.29 = (f32[256]{0:T(256)}, f32[256]{0:T(256)S(1)}, u32[]{:S(2)}) copy-start(f32[256]{0:T(256)S(1)} %add_rsqrt_fusion.1) | copy-start | bytes 3076
  40.6 64.5 %copy-start.17 = (bf16[256,768]{1,0:T(8,128)(2,1)}, bf16[256,768]{1,0:T(8,128)(2,1)S(1)}, u32[]{:S(2)}) copy-start(bf16[256,768]{1,0:T(8,128)(2,1)S(1)} %fusion.39) | copy-start | bytes 1179652
  73.4 26.1 %collective-permute-start.1 = (bf16[256,1536]{1,0:T(8,128)(2,1)S(1)}, bf16[256,1536]{1,0:T(8,128)(2,1)}, u32[]{:S(2)}, u32[]{:S(2)}) collective-permute-start(bf16[256,1536]{1,0:T(8,128)(2,1)S(1)} %slice.100), channel_id=1, source_target_pairs={{0,8},{4,12},{8,0},{12,4},{1,9},{5,13},{9,1},{13,5},{2,10},{6,14},... | collective-permute-start | bytes 2359304 | tf_op jit(solution)/shard_map/ppermute | solution.py:258
  74.7 24.9 %collective-permute-start = (bf16[256,1536]{1,0:T(8,128)(2,1)S(1)}, bf16[256,1536]{1,0:T(8,128)(2,1)}, u32[]{:S(2)}, u32[]{:S(2)}) collective-permute-start(bf16[256,1536]{1,0:T(8,128)(2,1)S(1)} %slice.100), channel_id=1, source_target_pairs={{0,4},{4,0},{8,12},{12,8},{1,5},{5,1},{9,13},{13,9},{2,6},{6,2},{1... | collective-permute-start | bytes 2359304 | tf_op jit(solution)/shard_map/ppermute | solution.py:258
  99.6 3.8 collective-permute-start.2
  105.1 16.3 %copy-start = (bf16[1024,1536]{1,0:T(8,128)(2,1)}, bf16[1024,1536]{1,0:T(8,128)(2,1)S(1)}, u32[]{:S(2)}) copy-start(bf16[1024,1536]{1,0:T(8,128)(2,1)S(1)} %pad_maximum_fusion.1.k_ref.v_ref) | copy-start | bytes 9437188
  122.5 50.3 %copy-start.13 = (bf16[256,768]{1,0:T(8,128)(2,1)}, bf16[256,768]{1,0:T(8,128)(2,1)S(1)}, u32[]{:S(2)}) copy-start(bf16[256,768]{1,0:T(8,128)(2,1)S(1)} %multiply_convert_fusion.2) | copy-start | bytes 1179652
  124.0 33.5 %all-to-all-start.1 = ((bf16[4,192,768]{2,1,0:T(8,128)(2,1)}), bf16[4,192,768]{2,1,0:T(8,128)(2,1)S(1)}, u32[]{:S(2)}, u32[]{:S(2)}) async-start(bf16[4,192,768]{2,1,0:T(8,128)(2,1)} %bitcast.118), calls=%async_computation.1 | async-start | bytes 2359296 | tf_op jit(solution)/shard_map/all_to_all | solution.py:285
  157.5 15.3 %copy-start.21 = (bf16[4,192,768]{2,1,0:T(8,128)(2,1)}, bf16[4,192,768]{2,1,0:T(8,128)(2,1)S(1)}, u32[]{:S(2)}) copy-start(bf16[4,192,768]{2,1,0:T(8,128)(2,1)S(1)} %all-to-all-done.1) | copy-start | bytes 3538948
  158.2 23.2 %all-to-all-start.3 = ((f32[4,1,192]{2,1,0:T(1,128)}), f32[4,1,192]{2,1,0:T(1,128)S(1)}, u32[]{:S(2)}, u32[]{:S(2)}) async-start(f32[4,1,192]{2,1,0:T(1,128)} %all_to_all.24), calls=%async_computation.3 | async-start | bytes 8192 | tf_op jit(solution)/shard_map/all_to_all | solution.py:354
  181.4 39.9 %all-to-all-start.2 = ((bf16[4,192,768]{2,1,0:T(8,128)(2,1)}), bf16[4,192,768]{2,1,0:T(8,128)(2,1)S(1)}, u32[]{:S(2)}, u32[]{:S(2)}) async-start(bf16[4,192,768]{2,1,0:T(8,128)(2,1)} %bitcast.117), calls=%async_computation.2 | async-start | bytes 2359296 | tf_op jit(solution)/shard_map/all_to_all | solution.py:285
  186.2 129.5 %reduce-scatter.3.cloned.1.call-start = ((), (), s32[]{:S(2)}) async-start(), calls=%async_computation.11 | async-start | bytes 10616832 | tf_op jit(solution)/shard_map/reduce_scatter | solution.py:415
  199.3 7.3 %copy-start.22 = (bf16[4,192,768]{2,1,0:T(8,128)(2,1)S(1)}, bf16[4,192,768]{2,1,0:T(8,128)(2,1)}, u32[]{:S(2)}) copy-start(bf16[4,192,768]{2,1,0:T(8,128)(2,1)} %copy-done.21) | copy-start | bytes 3538948
  221.4 32.3 %all-to-all-start.4 = ((bf16[4,192,768]{2,1,0:T(8,128)(2,1)}), bf16[4,192,768]{2,1,0:T(8,128)(2,1)}, u32[]{:S(2)}, u32[]{:S(2)}) async-start(bf16[4,192,768]{2,1,0:T(8,128)(2,1)} %bitcast.116), calls=%async_computation.4 | async-start | bytes 2359296 | tf_op jit(solution)/shard_map/all_to_all | solution.py:285
  226.6 148.0 %reduce-scatter.5.cloned.1.call-start = ((), (), s32[]{:S(2)}) async-start(), calls=%async_computation.12 | async-start | bytes 5529600 | tf_op jit(solution)/shard_map/reduce_scatter | solution.py:427
  228.6 29.5 %copy-start.26 = (f32[256,4]{0,1:T(4,128)}, f32[256,4]{0,1:T(4,128)S(1)}, u32[]{:S(2)}) copy-start(f32[256,4]{0,1:T(4,128)S(1)} %select_reduce_fusion) | copy-start | bytes 12292
  287.4 3.4 collective-permute-start.4
  287.4 9.5 %collective-permute-start.3 = (bf16[2,256,768]{2,1,0:T(8,128)(2,1)}, bf16[2,256,768]{2,1,0:T(8,128)(2,1)}, u32[]{:S(2)}, u32[]{:S(2)}) collective-permute-start(bf16[2,256,768]{2,1,0:T(8,128)(2,1)} %get-tuple-element.103), channel_id=1, source_target_pairs={{0,4},{4,0},{8,12},{12,8},{1,5},{5,1},{9,13},{13,9},{2,6},{6,2},{1... | collective-permute-start | bytes 2359304 | tf_op jit(solution)/shard_map/ppermute | solution.py:258
  291.9 22.0 %collective-permute-start.5 = (bf16[2,256,768]{2,1,0:T(8,128)(2,1)}, bf16[2,256,768]{2,1,0:T(8,128)(2,1)}, u32[]{:S(2)}, u32[]{:S(2)}) collective-permute-start(bf16[2,256,768]{2,1,0:T(8,128)(2,1)} %fusion.22), channel_id=1, source_target_pairs={{0,8},{4,12},{8,0},{12,4},{1,9},{5,13},{9,1},{13,5},{2,10},{6,14},... | collective-permute-start | bytes 2359304 | tf_op jit(solution)/shard_map/ppermute | solution.py:258
  294.2 21.4 %copy-start.5 = (bf16[256,768]{1,0:T(8,128)(2,1)S(1)}, bf16[256,768]{1,0:T(8,128)(2,1)}, u32[]{:S(2)}) copy-start(bf16[256,768]{1,0:T(8,128)(2,1)} %copy-done.4) | copy-start | bytes 1179652
  296.9 18.8 %copy-start.18 = (bf16[256,768]{1,0:T(8,128)(2,1)S(1)}, bf16[256,768]{1,0:T(8,128)(2,1)}, u32[]{:S(2)}) copy-start(bf16[256,768]{1,0:T(8,128)(2,1)} %copy-done.17) | copy-start | bytes 1179652
  320.6 58.6 %copy-start.11 = (f32[256,768]{1,0:T(8,128)S(1)}, f32[256,768]{1,0:T(8,128)}, u32[]{:S(2)}) copy-start(f32[256,768]{1,0:T(8,128)} %copy-done.10) | copy-start | bytes 2359300
  320.6 60.8 %copy-start.20 = (bf16[96,6144]{1,0:T(8,128)(2,1)S(1)}, bf16[96,6144]{1,0:T(8,128)(2,1)}, u32[]{:S(2)}) copy-start(bf16[96,6144]{1,0:T(8,128)(2,1)} %reduce-scatter.3.cloned.1.call-done) | copy-start | bytes 3538948
  374.6 21.0 %all-to-all-start.5 = ((bf16[4,24,3200]{2,1,0:T(8,128)(2,1)}), bf16[4,24,3200]{2,1,0:T(8,128)(2,1)S(1)}, u32[]{:S(2)}, u32[]{:S(2)}) async-start(bf16[4,24,3200]{2,1,0:T(8,128)(2,1)} %bitcast.119), calls=%async_computation.7 | async-start | bytes 1228800 | tf_op jit(solution)/shard_map/all_to_all | solution.py:285
  (17 other events, 48.2 us)
Sparse Core Ops, SparseCore 0:
  27.9 41.3 all-gather.3
  71.1 45.4 all-gather.5
  118.6 38.9 all-gather.7
  221.5 78.9 reduce-scatter.2
  319.6 54.9 reduce-scatter.4
